TPU v7x, 32 devices: a whole 2x2x4 slice. The times are simulated.
32 devices in a mesh: freq: 8 (over z, y), dish: 4 (over x, core).
Axes of the slice: x: 2, y: 2, z: 4, core: 2. Of those that a mesh axis runs over, the one named last changes fastest.
Arguments:
- voltages: bfloat16 [256, 4, 2, 155648], P('freq', 'dish'), may hold values from -6 to 6
- feed_gains: bfloat16 [256, 4, 2, 8192], P('freq', 'dish'), may hold values from -4.1875 to 4.1875
- block_assign: int32 [8], replicated, may hold values from 0 to 7, each once
- grid_rows: int32 [4, 256], replicated, may hold values from 0 to 255, each once within a row
Outputs:
- beam_power: float32 [8192, 1024], P('freq', 'dish')
Inputs may be any that keep to these rules, and one draw needn't show every extreme that they name: block_assign names every channel block once. Each row of grid_rows names every grid row once.
All inputs are finite; a program needn't handle non-finite values.
Results may differ from a plain program's by a relative error of at most 0.0042.
Values may be sent and summed in bfloat16 or wider, within the bound.
A program may use at most 192 MiB of HBM per device.

v0:
```python
import math

import jax
import jax.numpy as jnp
from jax import lax
from jax.sharding import PartitionSpec as P

NCHAN = 8192
CHA = 64
CHB = 128
TAPS = 4
FRAMES = 16


full_turn = 2.0 * math.pi


def swapped(shard, axis, distance):
    return lax.ppermute(shard, axis, [(i, i ^ 1 << distance) for i in range(lax.axis_size(axis))])


def fourier_table(row_index, col_index, modulus, scaling):
    phases = row_index[:, None] * col_index[None, :] % modulus
    angles = full_turn / modulus * phases.astype(jnp.float32)
    cosine_table = (jnp.cos(angles) * scaling).astype(jnp.bfloat16)
    sine_table = (jnp.sin(angles) * scaling).astype(jnp.bfloat16)
    upper_rows = jnp.stack([cosine_table, -sine_table], axis=1)
    lower_rows = jnp.stack([sine_table, cosine_table], axis=1)
    return jnp.stack([upper_rows, lower_rows], axis=0)


def rotate(real_part, imag_part, angles):
    cosine_part = jnp.cos(angles)
    sine_part = jnp.sin(angles)
    return (
        real_part * cosine_part - imag_part * sine_part,
        real_part * sine_part + imag_part * cosine_part,
    )


def filter_window():
    sample_index = jnp.arange(TAPS * NCHAN, dtype=jnp.float32)
    centred = (sample_index - TAPS * NCHAN / 2 + 0.5) / NCHAN
    taper_curve = 0.5 - 0.5 * jnp.cos(full_turn * (sample_index + 0.5) / (TAPS * NCHAN))
    shaped_window = (jnp.sinc(centred) * taper_curve).reshape(TAPS, NCHAN)
    energy = jnp.mean(jnp.sum(shaped_window * shaped_window, axis=0))
    return shaped_window / jnp.sqrt(energy)


def channelize(dish_volts, dish_gains):
    dish_rows = dish_volts.shape[0]
    window = filter_window()
    framed = dish_volts.reshape(dish_rows, 2, FRAMES + TAPS - 1, NCHAN)
    filtered = window[0] * framed[:, :, 0:FRAMES]
    for tap_index in range(1, TAPS):
        filtered = filtered + window[tap_index] * framed[:, :, tap_index : tap_index + FRAMES]
    filtered = filtered.astype(jnp.bfloat16)
    blocks = filtered.reshape(dish_rows, 2, FRAMES, CHA, CHB)
    first_index = jnp.arange(CHA, dtype=jnp.int32)
    second_index = jnp.arange(CHB, dtype=jnp.int32)
    first_table = fourier_table(first_index, first_index, CHA, 1.0 / math.sqrt(CHA))
    section_one = jnp.einsum(
        "rpfab,paqc->rfqcb", blocks, first_table, preferred_element_type=jnp.float32
    )
    angles = -(full_turn / NCHAN) * (first_index[:, None] * second_index[None, :] % NCHAN).astype(
        jnp.float32
    )
    real_part, imag_part = rotate(section_one[:, :, 0], section_one[:, :, 1], angles)
    turned = jnp.stack([real_part, imag_part], axis=2).astype(jnp.bfloat16)
    second_table = fourier_table(second_index, second_index, CHB, 1.0 / math.sqrt(CHB))
    spectrum = jnp.einsum(
        "rfqcb,qbse->rfsec", turned, second_table, preferred_element_type=jnp.float32
    )
    spectrum = spectrum.reshape(dish_rows, FRAMES, 2, NCHAN)
    gain_real = dish_gains[:, 0][:, None, :].astype(jnp.float32)
    gain_imag = dish_gains[:, 1][:, None, :].astype(jnp.float32)
    spectrum_real = spectrum[:, :, 0]
    spectrum_imag = spectrum[:, :, 1]
    out_real = spectrum_real * gain_real - spectrum_imag * gain_imag
    out_imag = spectrum_real * gain_imag + spectrum_imag * gain_real
    return jnp.stack([out_real, out_imag], axis=2).astype(jnp.bfloat16)


def body(voltages, feed_gains, block_assign, grid_rows):
    dish_rows = voltages.shape[0]
    channelized = channelize(voltages[:, 0], feed_gains[:, 0])
    block_count = lax.axis_size("freq")
    block_width = NCHAN // block_count
    ordered = jnp.take(
        channelized.reshape(dish_rows, FRAMES, 2, block_count, block_width), block_assign, axis=3
    )
    dish_count = lax.axis_size("dish")
    bit_count = dish_count.bit_length() - 1
    position = lax.axis_index("dish")
    gathered = lax.all_to_all(ordered, "freq", split_axis=3, concat_axis=0, tiled=True)[:, :, :, 0]
    grid_len = gathered.shape[0]
    total_dishes = grid_len * dish_count
    positions = jnp.arange(grid_len, dtype=jnp.int32)
    grid_order = lax.dynamic_index_in_dim(grid_rows, position, 0, keepdims=False)
    grid_table = fourier_table(grid_order, positions, grid_len, 1.0 / math.sqrt(grid_len))
    local_sums = jnp.einsum(
        "mfpc,pmqk->fcqk", gathered, grid_table, preferred_element_type=jnp.float32
    )
    twist_angles = -(full_turn / total_dishes) * (position * positions % total_dishes).astype(
        jnp.float32
    )
    real_part, imag_part = rotate(local_sums[:, :, 0], local_sums[:, :, 1], twist_angles)
    current = jnp.stack([real_part, imag_part], axis=2).astype(jnp.bfloat16)
    for section_index in range(bit_count):
        pair_bit = bit_count - 1 - section_index
        half_size = 1 << pair_bit
        if section_index == 0:
            partner = swapped(current, "dish", pair_bit)
        else:
            partner = swapped(current, "dish", pair_bit)
        own_part = lax.optimization_barrier(current).astype(jnp.float32)
        other_part = partner.astype(jnp.float32)
        upper_half = jnp.right_shift(position, pair_bit) % 2
        offset = position % half_size
        angles = -(full_turn / (2 * half_size)) * offset.astype(jnp.float32)
        difference = other_part - own_part
        real_part, imag_part = rotate(difference[:, :, 0], difference[:, :, 1], angles)
        current = jnp.where(
            upper_half == 0, own_part + other_part, jnp.stack([real_part, imag_part], axis=2)
        )
    beam_real = current[:, :, 0]
    beam_imag = current[:, :, 1]
    return jnp.mean(beam_real * beam_real + beam_imag * beam_imag, axis=0) / dish_count


def solution(mesh):
    placed = (P("freq", "dish", None, None), P("freq", "dish", None, None), P(), P())
    return jax.shard_map(
        body, mesh=mesh, in_specs=placed, out_specs=P("freq", "dish"), check_vma=False
    )
```

profile of v0, /device:TPU:0, one launch (start us, length us, event | category | flops | bytes accessed | tf_op | source)
XLA Modules:
  0.0 1411.3 jit_solution(12810824846196254972)
XLA Ops:
  0.0 1.2 fusion.43
  1.2 1.2 compare_and_fusion
  2.5 0.7 compare_select_fusion
  3.1 0.1 fusion.73
  3.3 0.3 fusion.72
  3.6 0.2 multiply_convert_fusion.4
  3.9 0.3 multiply_convert_fusion.2
  4.9 0.6 pad_clamp_fusion
  5.4 1.3 fusion.35
  6.8 6.7 slice_convert_fusion.1
  13.5 18.2 %copy.12 = bf16[32,1,2,155648]{3,0,2,1:T(8,128)(2,1)} copy(bf16[32,1,2,155648]{3,2,1,0:T(2,128)(2,1)} %param.4) | data formatting | bytes 39845888 | tf_op args[0]
  31.6 21.7 %reshape_squeeze.3 = bf16[32,2,19,8192]{3,2,0,1:T(8,128)(2,1)} reshape(bf16[32,1,2,155648]{3,0,2,1:T(8,128)(2,1)} %copy.12) | data formatting | bytes 39845888 | tf_op jit(solution)/shard_map/reshape;squeeze | solution.py:53
  53.4 35.3 %add_convert_fusion = bf16[32,2,16,8192]{3,2,0,1:T(8,128)(2,1)S(1)} fusion(bf16[32,2,19,8192]{3,2,0,1:T(8,128)(2,1)} %reshape_squeeze.3, f32[8192]{0:T(1024)S(1)} %bitcast.108, f32[8192]{0:T(1024)S(1)} %bitcast.109, f32[8192]{0:T(1024)S(1)} %bitcast.110, f32[8192]{0:T(1024)S(1)} %bitcast.107), kind=kLoop, calls=%fused_computation.6 | loop fusion | flops 100663296 | bytes 84017152 | tf_op jit(solution)/shard_map/convert_element_type | solution.py:57
  88.7 8.4 copy.31
  97.2 16.7 %convolution_bitcast_fusion.1 = f32[32,16,2,64,128]{4,3,1,0,2:T(8,128)} fusion(bf16[32,2,16,64,128]{4,3,2,0,1:T(8,128)(2,1)} %bitcast.98, bf16[1,64,2,64]{1,3,0,2:T(8,128)(2,1)S(1)} %get-tuple-element.28, bf16[1,64,2,64]{1,3,0,2:T(8,128)(2,1)S(1)} %get-tuple-element.27), kind=kOutput, calls=%fused_computation.8 | convolution fusion | flops 2147549184 | bytes 50364416 | tf_op jit(solution)/shard_map/rpfab,paqc->rfqcb/dot_general | solution.py:62
  113.9 15.1 %subtract_convert_fusion.2 = (bf16[32,16,1,64,128]{4,3,1,0,2:T(8,128)(2,1)S(1)}, bf16[32,16,1,64,128]{4,3,1,0,2:T(8,128)(2,1)}) fusion(f32[32,16,2,64,128]{4,3,1,0,2:T(8,128)} %convolution_bitcast_fusion.1, f32[64,128]{1,0:T(8,128)S(1)} %get-tuple-element.33, f32[64,128]{1,0:T(8,128)S(1)} %get-tuple-element.34), kind=kLoop, calls=%fused_computation.31 | loop fusion | flops 33554432 | bytes 50397184 | tf_op jit(solution)/shard_map/convert.8
  129.1 14.9 %convolution_bitcast_fusion = f32[32,16,2,128,64]{3,4,1,0,2:T(8,128)} fusion(bf16[1,128,2,128]{3,1,0,2:T(8,128)(2,1)S(1)} %get-tuple-element.26, bf16[1,128,2,128]{3,1,0,2:T(8,128)(2,1)S(1)} %get-tuple-element.25, bf16[32,16,1,64,128]{4,3,1,0,2:T(8,128)(2,1)} %get-tuple-element.8, bf16[32,16,1,64,128]{4,3,1,0,2:T(8,128)(2,1)S(1)} %get-tuple-element.7), kind=kOutput, calls=%fused_computation.7 | convolution fusion | flops 4303618048 | bytes 50462720 | tf_op jit(solution)/shard_map/rfqcb,qbse->rfsec/dot_general | solution.py:71
  144.0 44.5 %copy.15 = f32[32,16,2,128,64]{4,3,1,2,0:T(8,128)} copy(f32[32,16,2,128,64]{3,4,1,0,2:T(8,128)} %convolution_bitcast_fusion) | data formatting | bytes 67108864 | tf_op jit(solution)/shard_map/rfqcb,qbse->rfsec/transpose | solution.py:71
  188.5 55.0 %reshape.420 = f32[32,16,2,8192]{3,1,2,0:T(8,128)} reshape(f32[32,16,2,128,64]{4,3,1,2,0:T(8,128)} %copy.15) | data formatting | bytes 67108864 | tf_op jit(solution)/shard_map/reshape | solution.py:74
  243.5 1.2 copy_bitcast_fusion
  244.7 18.0 %add_convert_fusion.2 = (bf16[32,16,1,8192]{3,1,2,0:T(8,128)(2,1)}, bf16[32,16,1,8192]{3,1,2,0:T(8,128)(2,1)}) fusion(f32[32,16,2,8192]{3,1,2,0:T(8,128)} %reshape.420, f32[32,8192]{1,0:T(8,128)S(1)} %get-tuple-element.37, f32[32,8192]{1,0:T(8,128)S(1)} %get-tuple-element.38), kind=kLoop, calls=%fused_computation.28 | loop fusion | flops 33554432 | bytes 52428800 | tf_op jit(solution)/shard_map/convert.6
  262.7 16.3 %copy.33 = bf16[64,8,8,1024]{3,2,1,0:T(8,128)(2,1)} copy(bf16[64,8,8,1024]{3,1,2,0:T(8,128)(2,1)} %bitcast.102) | data formatting | bytes 16777216
  279.1 16.5 %copy.32 = bf16[64,8,8,1024]{3,2,1,0:T(8,128)(2,1)} copy(bf16[64,8,8,1024]{3,1,2,0:T(8,128)(2,1)} %bitcast.101) | data formatting | bytes 16777216
  295.6 11.8 copy_dynamic-update-slice_fusion.1
  307.4 11.3 copy_dynamic-update-slice_fusion
  318.7 11.9 fusion.82
  330.6 8.2 gather_fusion
  338.8 8.2 gather_fusion.1
  347.0 15.6 %maximum_select_fusion.1 = bf16[32,16,2,8,1024]{4,0,2,1,3:T(8,128)(2,1)} fusion(bf16[32,16,2,8,512]{4,0,2,1,3:T(8,128)(2,1)} %bitcast.100, bf16[32,16,2,8,512]{4,0,2,1,3:T(8,128)(2,1)} %bitcast.99, pred[8]{0:T(512)(128)(4,1)S(1)} %copy-done.4), kind=kLoop, calls=%fused_computation.14 | loop fusion | flops 41943040 | bytes 33554440 | tf_op jit(solution)/shard_map/jit(_take)/select_n | solution.py:89
  362.5 7.3 all-to-all-start
  369.9 1.1 fusion.57
  371.0 1.3 multiply_convert_fusion
  372.3 360.6 %all-to-all-done = bf16[32,16,2,8,1024]{4,0,2,1,3:T(8,128)(2,1)} async-done(((bf16[32,16,2,8,1024]{4,0,2,1,3:T(8,128)(2,1)}), bf16[32,16,2,8,1024]{4,0,2,1,3:T(8,128)(2,1)}, u32[]{:S(2)}, u32[]{:S(2)}) %all-to-all-start) | async-done | bytes 16777248 | tf_op jit(solution)/shard_map/all_to_all | solution.py:95
  732.9 18.6 %copy.18 = bf16[8,32,16,2,1,1024]{5,2,4,3,1,0:T(8,128)(2,1)} copy(bf16[8,32,16,2,1,1024]{5,1,3,2,0,4:T(8,128)(2,1)} %bitcast.27) | data formatting | bytes 33554432 | tf_op jit(solution)/shard_map/all_to_all | solution.py:95
  751.5 49.5 %fusion.9 = f32[16,1024,2,256]{3,1,2,0:T(8,128)} fusion(bf16[256,16,2,1024,1]{3,1,2,0,4:T(8,128)(2,1)} %bitcast.105, bf16[1,256,2,256]{3,1,0,2:T(8,128)(2,1)S(1)} %get-tuple-element.20, bf16[1,256,2,256]{3,1,0,2:T(8,128)(2,1)S(1)} %get-tuple-element.19), kind=kOutput, calls=%fused_computation.32 | convolution fusion | flops 8590983168 | bytes 50855936 | tf_op jit(solution)/shard_map/mfpc,pmqk->fcqk/dot_general | solution.py:101
  801.0 12.1 subtract_convert_fusion
  813.2 6.8 pad_maximum_fusion.1
  820.0 1.5 collective-permute-start
  821.6 359.6 %collective-permute-done = bf16[16,1024,2,256]{3,1,2,0:T(8,128)(2,1)} collective-permute-done((bf16[16,1024,2,256]{3,1,2,0:T(8,128)(2,1)}, bf16[16,1024,2,256]{3,1,2,0:T(8,128)(2,1)}, u32[]{:S(2)}, u32[]{:S(2)}) %collective-permute-start) | collective-permute-done | bytes 16777248 | tf_op jit(solution)/shard_map/ppermute | solution.py:19
  1181.2 23.1 %convert_subtract_fusion = f32[16,1024,2,256]{3,1,2,0:T(8,128)} fusion(bf16[16,1024,2,256]{3,1,2,0:T(8,128)(2,1)} %collective-permute-done, bf16[16,1024,2,256]{3,1,2,0:T(8,128)(2,1)} %pad_maximum_fusion.1), kind=kLoop, calls=%fused_computation.2 | loop fusion | flops 25165824 | bytes 67108864 | tf_op jit(solution)/shard_map/sub | solution.py:121
  1204.3 21.4 %multiply_subtract_fusion.1 = (f32[16,1024,1,256]{3,1,2,0:T(8,128)}, f32[16,1024,1,256]{3,1,2,0:T(8,128)}) fusion(f32[16,1024,2,256]{3,1,2,0:T(8,128)} %convert_subtract_fusion, f32[]{:T(128)S(6)} %sin.71, f32[]{:T(128)S(6)} %cos.68), kind=kLoop, calls=%fused_computation.25 | loop fusion | flops 25165824 | bytes 67108872 | tf_op jit(solution)/shard_map/sub | solution.py:36
  1225.7 33.3 %fusion = f32[16,1024,2,256]{3,1,2,0:T(8,128)} fusion(bf16[16,1024,2,256]{3,1,2,0:T(8,128)(2,1)} %collective-permute-done, bf16[16,1024,2,256]{3,1,2,0:T(8,128)(2,1)} %pad_maximum_fusion.1, f32[16,1024,1,256]{3,1,2,0:T(8,128)} %get-tuple-element.14, f32[16,1024,1,256]{3,1,2,0:T(8,128)} %get-tuple-element.13, pred[]{:T(512)S(6)} %eq.52), kind=kLoop, calls=%fused_computation.4 | loop fusion | flops 41943040 | bytes 100663296 | tf_op jit(solution)/shard_map/jit(_where)/select_n | solution.py:123
  1259.0 49.5 %collective-permute-done.1 = f32[16,1024,2,256]{3,1,2,0:T(8,128)} collective-permute-done((f32[16,1024,2,256]{3,1,2,0:T(8,128)}, f32[16,1024,2,256]{3,1,2,0:T(8,128)}, u32[]{:S(2)}, u32[]{:S(2)}) %collective-permute-start.1) | collective-permute-done | bytes 33554464 | tf_op jit(solution)/shard_map/ppermute | solution.py:19
  1308.5 33.4 %sub.62 = f32[16,1024,2,256]{3,1,2,0:T(8,128)} subtract(f32[16,1024,2,256]{3,1,2,0:T(8,128)} %collective-permute-done.1, f32[16,1024,2,256]{3,1,2,0:T(8,128)} %fusion) | non-fusion elementwise | flops 8388608 | bytes 100663296 | tf_op jit(solution)/shard_map/sub | solution.py:121
  1341.9 17.9 %multiply_subtract_fusion = (f32[16,1024,1,256]{3,1,2,0:T(8,128)S(1)}, f32[16,1024,1,256]{3,1,2,0:T(8,128)}) fusion(f32[16,1024,2,256]{3,1,2,0:T(8,128)} %sub.62), kind=kLoop, calls=%fused_computation.23 | loop fusion | flops 16777216 | bytes 67108864 | tf_op jit(solution)/shard_map/sub | solution.py:36
  1359.8 38.5 %maximum_select_fusion = f32[16,1024,2,256]{3,1,2,0:T(8,128)} fusion(f32[16,1024,1,256]{3,1,2,0:T(8,128)} %get-tuple-element.12, f32[16,1024,1,256]{3,1,2,0:T(8,128)S(1)} %get-tuple-element.11, f32[16,1024,2,256]{3,1,2,0:T(8,128)} %fusion, f32[16,1024,2,256]{3,1,2,0:T(8,128)} %collective-permute-done.1, pred[]{:T(512)S(6)} %eq.51), kind=kLoop, calls=%fused_computation.5 | loop fusion | flops 25165824 | bytes 134217728 | tf_op jit(solution)/shard_map/jit(_where)/select_n | solution.py:123
  1398.2 11.6 fusion.2
  1409.8 1.0 broadcast_multiply_fusion
  (18 shorter events, 0.4 us)
Async XLA Ops:
  0.0 369.8 %copy-start = (s32[4,256]{1,0:T(4,128)S(1)}, s32[4,256]{1,0:T(4,128)}, u32[]{:S(2)}) copy-start(s32[4,256]{1,0:T(4,128)} %param.7) | copy-start | bytes 12292
  188.5 55.0 %copy-start.2 = (f32[32,1,8192]{2,1,0:T(1,128)S(1)}, f32[32,1,8192]{2,1,0:T(1,128)}, u32[]{:S(2)}) copy-start(f32[32,1,8192]{2,1,0:T(1,128)} %get-tuple-element.17) | copy-start | bytes 3145732
  188.5 55.0 %copy-start.3 = (f32[32,1,8192]{2,1,0:T(1,128)S(1)}, f32[32,1,8192]{2,1,0:T(1,128)}, u32[]{:S(2)}) copy-start(f32[32,1,8192]{2,1,0:T(1,128)} %get-tuple-element.18) | copy-start | bytes 3145732
  330.6 16.4 %copy-start.4 = (pred[8]{0:T(512)(128)(4,1)S(1)}, pred[8]{0:T(512)(128)(4,1)}, u32[]{:S(2)}) copy-start(pred[8]{0:T(512)(128)(4,1)} %compare_and_fusion) | copy-start | bytes 28
  362.5 370.3 %all-to-all-start = ((bf16[32,16,2,8,1024]{4,0,2,1,3:T(8,128)(2,1)}), bf16[32,16,2,8,1024]{4,0,2,1,3:T(8,128)(2,1)}, u32[]{:S(2)}, u32[]{:S(2)}) async-start(bf16[32,16,2,8,1024]{4,0,2,1,3:T(8,128)(2,1)} %maximum_select_fusion.1), calls=%async_computation | async-start | bytes 33554432 | tf_op jit(solution)/shard_map/all_to_all | solution.py:95
  820.0 361.2 %collective-permute-start = (bf16[16,1024,2,256]{3,1,2,0:T(8,128)(2,1)}, bf16[16,1024,2,256]{3,1,2,0:T(8,128)(2,1)}, u32[]{:S(2)}, u32[]{:S(2)}) collective-permute-start(bf16[16,1024,2,256]{3,1,2,0:T(8,128)(2,1)} %pad_maximum_fusion.1), channel_id=1, source_target_pairs={{0,2},{1,3},{2,0},{3,1},{4,6},{5,7},{6,4},{7,5},{8,10},{9,11},{10,... | collective-permute-start | bytes 50331656 | tf_op jit(solution)/shard_map/ppermute | solution.py:19
  1259.0 49.5 %collective-permute-start.1 = (f32[16,1024,2,256]{3,1,2,0:T(8,128)}, f32[16,1024,2,256]{3,1,2,0:T(8,128)}, u32[]{:S(2)}, u32[]{:S(2)}) collective-permute-start(f32[16,1024,2,256]{3,1,2,0:T(8,128)} %fusion), channel_id=1, source_target_pairs={{0,1},{1,0},{2,3},{3,2},{4,5},{5,4},{6,7},{7,6},{8,9},{9,8},{10,11... | collective-permute-start | bytes 100663304 | tf_op jit(solution)/shard_map/ppermute | solution.py:19
  1359.8 51.1 %copy-start.1 = (s32[4,256]{1,0:T(4,128)S(1)}, s32[4,256]{1,0:T(4,128)}, u32[]{:S(2)}) copy-start(s32[4,256]{1,0:T(4,128)} %param.7) | copy-start | bytes 12292
where the time goes:
time: 1420 us; the launch traced here: 1410 us
  waiting for transfers between devices  770 us (54%)
  other arithmetic  298 us (21%)
  local copies, waits for them, and re-layouts  252 us (18%)
  matrix products  81.1 us (6%)
    ppermute x2, waiting for transfers between devices, swapped(): lax.ppermute(shard, axis, [(i, i ^ 1 << distance) for i in range(lax.axis...  409 us
    all_to_all x1, waiting for transfers between devices, body(): lax.all_to_all(ordered, 'freq', split_axis=3, concat_axis=0, tiled=True)  361 us
    unnamed x16, local copies, waits for them, and re-layouts  72.5 us
    select_n x2, other arithmetic, body(): jnp.where(upper_half == 0, own_part + other_part, jnp.stack([real_part, i...  71.8 us
    sub x2, other arithmetic, body(): difference = other_part - own_part  56.5 us
    reshape x1, local copies, waits for them, and re-layouts, channelize(): spectrum = spectrum.reshape(dish_rows, FRAMES, 2, NCHAN)  55 us
    dot_general x1, matrix products, body(): jnp.einsum('mfpc,pmqk->fcqk', gathered, grid_table, preferred_element_typ...  49.5 us
    another operation x3, other arithmetic  45.3 us
  transfers between devices with their start and end apart: 3, of which 3 were waited for; matrix products, arithmetic and copies ran while one was open for 0% of the time, Pallas kernels for 0%

commit v1 on v0

v1 whole, which is shorter than its diff:
```python
import math

import jax
import jax.numpy as jnp
from jax import lax
from jax.experimental import pallas as pl
from jax.experimental.pallas import tpu as pltpu
from jax.sharding import PartitionSpec as P

NCHAN = 8192
CHA = 64
CHB = 128
TAPS = 4
FRAMES = 16
N_DISH = 4
CHUNKS = 4


full_turn = 2.0 * math.pi


def fourier_table(row_index, col_index, modulus, scaling):
    phases = row_index[:, None] * col_index[None, :] % modulus
    angles = full_turn / modulus * phases.astype(jnp.float32)
    cosine_table = (jnp.cos(angles) * scaling).astype(jnp.bfloat16)
    sine_table = (jnp.sin(angles) * scaling).astype(jnp.bfloat16)
    upper_rows = jnp.stack([cosine_table, -sine_table], axis=1)
    lower_rows = jnp.stack([sine_table, cosine_table], axis=1)
    return jnp.stack([upper_rows, lower_rows], axis=0)


def rotate(real_part, imag_part, angles):
    cosine_part = jnp.cos(angles)
    sine_part = jnp.sin(angles)
    return (
        real_part * cosine_part - imag_part * sine_part,
        real_part * sine_part + imag_part * cosine_part,
    )


def filter_window():
    sample_index = jnp.arange(TAPS * NCHAN, dtype=jnp.float32)
    centred = (sample_index - TAPS * NCHAN / 2 + 0.5) / NCHAN
    taper_curve = 0.5 - 0.5 * jnp.cos(full_turn * (sample_index + 0.5) / (TAPS * NCHAN))
    shaped_window = (jnp.sinc(centred) * taper_curve).reshape(TAPS, NCHAN)
    energy = jnp.mean(jnp.sum(shaped_window * shaped_window, axis=0))
    return shaped_window / jnp.sqrt(energy)


def channelize(framed, window, first_table, second_table, gains):
    frames = framed.shape[2] - TAPS + 1
    filtered = window[0] * framed[:, :, 0:frames]
    for tap_index in range(1, TAPS):
        filtered = filtered + window[tap_index] * framed[:, :, tap_index : tap_index + frames]
    filtered = filtered.astype(jnp.bfloat16)
    section_one = jnp.einsum(
        "rpfab,paqc->rfqcb", filtered, first_table, preferred_element_type=jnp.float32
    )
    first_index = jnp.arange(CHA, dtype=jnp.int32)
    second_index = jnp.arange(CHB, dtype=jnp.int32)
    angles = -(full_turn / NCHAN) * (first_index[:, None] * second_index[None, :] % NCHAN).astype(
        jnp.float32
    )
    real_part, imag_part = rotate(section_one[:, :, 0], section_one[:, :, 1], angles)
    turned = jnp.stack([real_part, imag_part], axis=2).astype(jnp.bfloat16)
    spectrum = jnp.einsum(
        "rfqcb,qbse->rfsec", turned, second_table, preferred_element_type=jnp.float32
    )
    spectrum_real = spectrum[:, :, 0]
    spectrum_imag = spectrum[:, :, 1]
    gain_real = gains[:, 0][:, None]
    gain_imag = gains[:, 1][:, None]
    out_real = spectrum_real * gain_real - spectrum_imag * gain_imag
    out_imag = spectrum_real * gain_imag + spectrum_imag * gain_real
    return jnp.stack([out_real, out_imag], axis=2).astype(jnp.bfloat16)


def beam_kernel(scale, x_ref, table_ref, twist_ref, power_ref):
    groups, _, _, _, rows, width = x_ref.shape
    positions = twist_ref.shape[2]
    parts = []
    for d in range(N_DISH):
        sums = None
        for p in range(2):
            feeds = x_ref[:, d, 0, p]
            if rows % 16:
                feeds = feeds.astype(jnp.float32).reshape(groups * rows, width).astype(jnp.bfloat16)
            else:
                feeds = feeds.reshape(groups * rows, width)
            term = lax.dot_general(
                feeds,
                table_ref[d, p],
                (((0,), (0,)), ((), ())),
                preferred_element_type=jnp.float32,
            )
            sums = term if sums is None else sums + term
        real, imag = sums[:, :positions], sums[:, positions:]
        cosine, sine = twist_ref[d, 0:1], twist_ref[d, 1:2]
        parts.append(
            (
                (real * cosine - imag * sine).astype(jnp.bfloat16).astype(jnp.float32),
                (real * sine + imag * cosine).astype(jnp.bfloat16).astype(jnp.float32),
            )
        )
    (r0, i0), (r1, i1), (r2, i2), (r3, i3) = parts
    ar, ai, br, bi = r0 + r2, i0 + i2, r1 + r3, i1 + i3
    cr, ci, dr, di = r0 - r2, i0 - i2, r1 - r3, i1 - i3
    beams = (
        (ar + br, ai + bi),
        (ar - br, ai - bi),
        (cr + di, ci - dr),
        (cr - di, ci + dr),
    )

    @pl.when(pl.program_id(0) == 0)
    def _():
        power_ref[...] = jnp.zeros_like(power_ref)

    for s, (real, imag) in enumerate(beams):
        power_ref[s] += (real * real + imag * imag) * scale


def beam_power(gathered, tables, twist):
    groups, dishes, frames, _, rows, width = gathered.shape
    positions = twist.shape[2]
    return pl.pallas_call(
        lambda *refs: beam_kernel(1.0 / (N_DISH * FRAMES), *refs),
        grid=(frames,),
        in_specs=[
            pl.BlockSpec((groups, dishes, 1, 2, rows, width), lambda f: (0, 0, f, 0, 0, 0)),
            pl.BlockSpec(tables.shape, lambda f: (0, 0, 0, 0)),
            pl.BlockSpec(twist.shape, lambda f: (0, 0, 0)),
        ],
        out_specs=pl.BlockSpec((N_DISH, width, positions), lambda f: (0, 0, 0)),
        out_shape=jax.ShapeDtypeStruct((N_DISH, width, positions), jnp.float32),
        compiler_params=pltpu.CompilerParams(vmem_limit_bytes=40 * 2**20),
        cost_estimate=pl.CostEstimate(
            flops=frames * dishes * groups * rows * 2 * width * positions * 4,
            bytes_accessed=gathered.size * 2 + tables.size * 2,
            transcendentals=0,
        ),
    )(gathered, tables, twist)


def body(voltages, feed_gains, block_assign, grid_rows):
    dish_rows = voltages.shape[0]
    block_count = lax.axis_size("freq")
    dish_count = lax.axis_size("dish")
    devices = block_count * dish_count
    block_width = NCHAN // block_count
    width = block_width // dish_count
    grid_len = grid_rows.shape[1]
    total_dishes = grid_len * dish_count

    window = filter_window().reshape(TAPS, CHA, CHB)
    first_index = jnp.arange(CHA, dtype=jnp.int32)
    second_index = jnp.arange(CHB, dtype=jnp.int32)
    first_table = fourier_table(first_index, first_index, CHA, 1.0 / math.sqrt(CHA))
    per_block = CHB // block_count
    ordered = (
        block_assign[:, None] * per_block + jnp.arange(per_block, dtype=jnp.int32)[None]
    ).reshape(CHB)
    second_table = fourier_table(second_index, ordered, CHB, 1.0 / math.sqrt(CHB))
    chosen = (jnp.arange(block_count)[:, None] == block_assign[None, :]).astype(jnp.bfloat16)
    gains = jnp.einsum(
        "rpbw,bn->rpnw",
        feed_gains[:, 0].reshape(dish_rows, 2, block_count, block_width),
        chosen,
        preferred_element_type=jnp.float32,
    ).reshape(dish_rows, 2, CHB, CHA)

    positions = jnp.arange(grid_len, dtype=jnp.int32)
    tables = jax.vmap(
        lambda line: fourier_table(line, positions, grid_len, 1.0 / math.sqrt(grid_len))
    )(grid_rows).reshape(dish_count, 2, grid_len, 2 * grid_len)
    classes = jnp.arange(dish_count, dtype=jnp.int32)
    twist_angles = -(full_turn / total_dishes) * (
        classes[:, None] * positions[None, :] % total_dishes
    ).astype(jnp.float32)
    twist = jnp.stack([jnp.cos(twist_angles), jnp.sin(twist_angles)], axis=1)

    framed = voltages[:, 0].reshape(dish_rows, 2, FRAMES + TAPS - 1, CHA, CHB)
    step = FRAMES // CHUNKS
    total = None
    for chunk in range(CHUNKS):
        piece = framed[:, :, chunk * step : chunk * step + step + TAPS - 1]
        spectra = channelize(piece, window, first_table, second_table, gains)
        spectra = spectra.reshape(dish_rows, step, 2, devices, width)
        sent = jnp.transpose(spectra, (3, 1, 2, 0, 4))
        gathered = lax.all_to_all(sent, ("freq", "dish"), split_axis=0, concat_axis=0, tiled=True)
        gathered = gathered.reshape(block_count, dish_count, step, 2, dish_rows, width)
        power = beam_power(gathered, tables, twist)
        total = power if total is None else total + power
    out = lax.all_to_all(total, "dish", split_axis=0, concat_axis=0, tiled=True)
    return out.reshape(block_width, grid_len)


def solution(mesh):
    placed = (P("freq", "dish", None, None), P("freq", "dish", None, None), P(), P())
    return jax.shard_map(
        body, mesh=mesh, in_specs=placed, out_specs=P("freq", "dish"), check_vma=False
    )
```

time: 1420 us -> 663 us (0.47)
  waiting for transfers between devices: 770 us -> 243 us
  other arithmetic: 298 us -> 63.5 us
  matrix products: 81.1 us -> 52.4 us
  Pallas kernels: 0 us -> 19.6 us
  local copies, waits for them, and re-layouts: 252 us -> 235 us
  blocking collectives: 0 us -> 16.9 us
    ppermute x2 -> x0, waiting for transfers between devices: 409 us -> none  [swapped(): lax.ppermute(shard, axis, [(i, i ^ 1 << distance) for i in range(lax.axis...]
    all_to_all x1 -> x4, waiting for transfers between devices: 361 us -> 243 us  [body(): lax.all_to_all(sent, ('freq', 'dish'), split_axis=0, concat_axis=0, tiled...]
    sub x4 -> x0, other arithmetic: 95.8 us -> none  [the longest x2 56.5 us: body(): difference = other_part - own_part]
    select_n x4 -> x0, other arithmetic: 88 us -> none  [the longest x2 71.8 us: body(): jnp.where(upper_half == 0, own_part + other_part, jnp.stack([real_part, i...]
    unnamed x16 -> x49, local copies, waits for them, and re-layouts: 72.5 us -> 9.07 us
    slice x1 -> x2, local copies, waits for them, and re-layouts: 0.09 us -> 55 us  [channelize(): filtered = window[0] * framed[:, :, 0:frames]]
    reshape x1 -> x2, local copies, waits for them, and re-layouts: 55 us -> 5.72 us  [the longest x1 3.15 us: body(): tables = jax.vmap(lambda line: fourier_table(line, positions, grid_len, 1...]
    another operation x1 -> x10, local copies, waits for them, and re-layouts: 21.7 us -> 67.7 us  [channelize(): framed = dish_volts.reshape(dish_rows, 2, FRAMES + TAPS - 1, NCHAN)]
  transfers between devices with their start and end apart: 3 -> 4, of which waited for: 3 -> 4; matrix products, arithmetic and copies ran while one was open for 0% -> 18% of each run, Pallas kernels for 0% -> 2%
where the time goes in v1:
time: 663 us; the launch traced here: 652 us
  waiting for transfers between devices  243 us (37%)
  local copies, waits for them, and re-layouts  235 us (35%)
  other arithmetic  63.5 us (10%)
  matrix products  52.4 us (8%)
  starting transfers between devices  20.2 us (3%)
  Pallas kernels  19.6 us (3%)
  blocking collectives  16.9 us (3%)
    all_to_all x4, waiting for transfers between devices, body(): lax.all_to_all(sent, ('freq', 'dish'), split_axis=0, concat_axis=0, tiled...  243 us
    slice x2, local copies, waits for them, and re-layouts, channelize(): filtered = window[0] * framed[:, :, 0:frames]  55 us
    another operation x8, local copies, waits for them, and re-layouts, channelize(): return jnp.stack([out_real, out_imag], axis=2).astype(jnp.bfloat16)  52.7 us
    another operation x2, other arithmetic  39.2 us
    another operation x8, local copies, waits for them, and re-layouts  36.7 us
    dot_general x4, matrix products, channelize(): jnp.einsum('rpfab,paqc->rfqcb', filtered, first_table, preferred_element_...  31.4 us
    another operation x1, local copies, waits for them, and re-layouts, body(): framed = voltages[:, 0].reshape(dish_rows, 2, FRAMES + TAPS - 1, CHA, CHB)  30.1 us
    transpose x4, local copies, waits for them, and re-layouts, body(): sent = jnp.transpose(spectra, (3, 1, 2, 0, 4))  20.9 us
  transfers between devices with their start and end apart: 4, of which 4 were waited for; matrix products, arithmetic and copies ran while one was open for 18% of the time, Pallas kernels for 2%

profile of v1, /device:TPU:0, one launch (start us, length us, event | category | flops | bytes accessed | tf_op | source)
XLA Modules:
  0.0 652.2 jit_solution(16624189700294398926)
XLA Ops:
  3.1 30.1 %reshape_squeeze.6 = bf16[32,2,19,64,128]{4,3,2,1,0:T(8,128)(2,1)} reshape(bf16[32,1,2,155648]{3,2,1,0:T(2,128)(2,1)} %param.4) | data formatting | bytes 39845888 | tf_op jit(solution)/shard_map/reshape;squeeze | solution.py:182
  33.2 54.3 %fusion.111 = (bf16[32,2,4,64,128]{4,3,2,1,0:T(8,128)(2,1)}, bf16[32,2,4,64,128]{4,3,2,1,0:T(8,128)(2,1)}, bf16[32,2,4,64,128]{4,3,2,1,0:T(8,128)(2,1)}, bf16[32...) fusion(bf16[32,2,19,64,128]{4,3,2,1,0:T(8,128)(2,1)} %reshape_s, ...), kind=kLoop, calls=%fused_computation.180 | loop fusion | bytes 134217728 | tf_op jit(solution)/shard_map/slice | solution.py:52
  94.1 4.0 slice_bitcast_fusion.1
  101.9 10.2 %fusion.36 = f32[32,4,2,64,128]{4,3,1,0,2:T(8,128)} fusion(bf16[32,2,4,64,128]{4,3,2,1,0:T(8,128)(2,1)} %get-tuple-element.16, bf16[32,2,4,64,128]{4,3,2,1,0:T(8,128)(2,1)} %get-tuple-element.17, bf16[32,2,4,64,128]{4,3,2,1,0:T(8,128)(2,1)} %get-tuple-element.18, bf16[32,2,4,64,128]{4,3,2,1,0:T(8,128)(2,1)} %get-tuple-element.19, ...), kind=kOutput, calls=%fused_computation.52 | convolution fusion | flops 562102272 | bytes 25329664 | tf_op jit(solution)/shard_map/rpfab,paqc->rfqcb/dot_general | solution.py:56
  115.6 6.4 fusion.45
  122.0 8.7 %fusion.42 = f32[32,4,2,64,128]{4,3,1,0,2:T(8,128)} fusion(bf16[32,2,4,64,128]{4,3,2,1,0:T(8,128)(2,1)S(1)} %copy-done.14, bf16[32,2,4,64,128]{4,3,2,1,0:T(8,128)(2,1)S(1)} %copy-done.15, bf16[32,2,4,64,128]{4,3,2,1,0:T(8,128)(2,1)} %get-tuple-element.11, bf16[32,2,4,64,128]{4,3,2,1,0:T(8,128)(2,1)} %get-tuple-element.12, f32[64,128]{1,0:T(8,128)S(1)} %bitcast.188, ...), kind=kOutput, calls=%fused_computation.54 | convolution fusion | flops 562102272 | bytes 25329664 | tf_op jit(solution)/shard_map/rpfab,paqc->rfqcb/dot_general | solution.py:56
  133.3 6.1 fusion.39
  139.4 19.4 %subtract_convert_fusion.5 = (bf16[32,4,1,64,128]{4,3,1,0,2:T(8,128)(2,1)S(1)}, bf16[32,4,1,64,128]{4,3,1,0,2:T(8,128)(2,1)}, bf16[32,4,1,64,128]{4,3,1,0,2:T(8,...) fusion(f32[32,4,2,64,128]{4,3,1,0,2:T(8,128)} %fusion.39, ...), kind=kLoop, calls=%fused_computation.39 | loop fusion | flops 33554432 | bytes 50397184 | tf_op jit(solution)/shard_map/convert.16
  158.8 6.9 %fusion.24 = f32[32,4,2,128,64]{3,4,1,0,2:T(8,128)} fusion(bf16[1,128,2,128]{3,1,0,2:T(8,128)(2,1)S(1)} %get-tuple-element.58, bf16[1,128,2,128]{3,1,0,2:T(8,128)(2,1)S(1)} %get-tuple-element.57, bf16[32,4,1,64,128]{4,3,1,0,2:T(8,128)(2,1)} %get-tuple-element.55, bf16[32,4,1,64,128]{4,3,1,0,2:T(8,128)(2,1)} %get-tuple-element.56), kind=kOutput, calls=%fused_computation.48 | convolution fusion | flops 1076101120 | bytes 12713984 | tf_op jit(solution)/shard_map/rfqcb,qbse->rfsec/dot_general | solution.py:66
  165.8 4.5 fusion.33
  170.3 4.5 fusion.30
  174.8 4.5 fusion.27
  179.3 19.8 %subtract_convert_fusion.4 = (bf16[32,4,1,128,64]{3,4,1,0,2:T(8,128)(2,1)}, bf16[32,4,1,128,64]{3,4,1,0,2:T(8,128)(2,1)}, bf16[32,4,1,128,64]{3,4,1,0,2:T(8,128)...) fusion(f32[32,4,2,128,64]{3,4,1,0,2:T(8,128)} %fusion.27, ...), kind=kLoop, calls=%fused_computation.37 | loop fusion | flops 33554432 | bytes 52428800 | tf_op jit(solution)/shard_map/convert.15
  199.1 4.8 copy.128
  203.9 6.6 %stack.143 = bf16[32,4,1,32,256]{4,3,1,0,2:T(8,128)(2,1)} reshape(bf16[32,4,1,128,64]{4,3,1,0,2:T(8,128)(2,1)} %copy.128) | data formatting | bytes 4194304 | tf_op jit(solution)/shard_map/stack | solution.py:75
  210.5 4.8 copy.129
  215.3 6.7 %stack.144 = bf16[32,4,1,32,256]{4,3,1,0,2:T(8,128)(2,1)} reshape(bf16[32,4,1,128,64]{4,3,1,0,2:T(8,128)(2,1)} %copy.129) | data formatting | bytes 4194304 | tf_op jit(solution)/shard_map/stack | solution.py:75
  224.6 5.3 copy.130
  229.9 7.4 %all-to-all-start.1 = ((bf16[32,4,2,32,256]{4,1,3,2,0:T(4,128)(2,1)}), bf16[32,4,2,32,256]{4,1,3,2,0:T(4,128)(2,1)}, u32[]{:S(2)}, u32[]{:S(2)}) async-start(bf16[32,4,2,32,256]{4,1,3,2,0:T(4,128)(2,1)} %copy.130), calls=%async_computation.1 | async-start | bytes 8388608 | tf_op jit(solution)/shard_map/all_to_all | solution.py:190
  237.3 4.8 copy.117
  242.2 6.6 %stack.133 = bf16[32,4,1,32,256]{4,3,1,0,2:T(8,128)(2,1)} reshape(bf16[32,4,1,128,64]{4,3,1,0,2:T(8,128)(2,1)} %copy.117) | data formatting | bytes 4194304 | tf_op jit(solution)/shard_map/stack | solution.py:75
  248.7 4.8 copy.118
  253.5 6.5 %stack.134 = bf16[32,4,1,32,256]{4,3,1,0,2:T(8,128)(2,1)} reshape(bf16[32,4,1,128,64]{4,3,1,0,2:T(8,128)(2,1)} %copy.118) | data formatting | bytes 4194304 | tf_op jit(solution)/shard_map/stack | solution.py:75
  262.7 5.3 copy.119
  267.9 63.3 %all-to-all-done.1 = bf16[32,4,2,32,256]{4,1,3,2,0:T(4,128)(2,1)} async-done(((bf16[32,4,2,32,256]{4,1,3,2,0:T(4,128)(2,1)}), bf16[32,4,2,32,256]{4,1,3,2,0:T(4,128)(2,1)}, u32[]{:S(2)}, u32[]{:S(2)}) %all-to-all-start.1) | async-done | bytes 4194336 | tf_op jit(solution)/shard_map/all_to_all | solution.py:190
  331.2 4.5 all-to-all-start
  335.7 4.8 copy.137
  340.5 6.5 %stack.147 = bf16[32,4,1,32,256]{4,3,1,0,2:T(8,128)(2,1)} reshape(bf16[32,4,1,128,64]{4,3,1,0,2:T(8,128)(2,1)} %copy.137) | data formatting | bytes 4194304 | tf_op jit(solution)/shard_map/stack | solution.py:75
  347.0 4.8 copy.138
  351.8 6.5 %stack.148 = bf16[32,4,1,32,256]{4,3,1,0,2:T(8,128)(2,1)} reshape(bf16[32,4,1,128,64]{4,3,1,0,2:T(8,128)(2,1)} %copy.138) | data formatting | bytes 4194304 | tf_op jit(solution)/shard_map/stack | solution.py:75
  361.0 5.2 copy.139
  366.1 63.5 %all-to-all-done = bf16[32,4,2,32,256]{4,1,3,2,0:T(4,128)(2,1)} async-done(((bf16[32,4,2,32,256]{4,1,3,2,0:T(4,128)(2,1)}), bf16[32,4,2,32,256]{4,1,3,2,0:T(4,128)(2,1)}, u32[]{:S(2)}, u32[]{:S(2)}) %all-to-all-start) | async-done | bytes 4194336 | tf_op jit(solution)/shard_map/all_to_all | solution.py:190
  429.6 4.0 all-to-all-start.2
  433.7 4.8 copy.146
  438.5 6.6 %stack.151 = bf16[32,4,1,32,256]{4,3,1,0,2:T(8,128)(2,1)} reshape(bf16[32,4,1,128,64]{4,3,1,0,2:T(8,128)(2,1)} %copy.146) | data formatting | bytes 4194304 | tf_op jit(solution)/shard_map/stack | solution.py:75
  448.2 6.7 %stack.152 = bf16[32,4,1,32,256]{4,3,1,0,2:T(8,128)(2,1)} reshape(bf16[32,4,1,128,64]{4,3,1,0,2:T(8,128)(2,1)} %copy.147) | data formatting | bytes 4194304 | tf_op jit(solution)/shard_map/stack | solution.py:75
  456.9 5.2 copy.148
  462.1 65.4 %all-to-all-done.2 = bf16[32,4,2,32,256]{4,1,3,2,0:T(4,128)(2,1)} async-done(((bf16[32,4,2,32,256]{4,1,3,2,0:T(4,128)(2,1)}), bf16[32,4,2,32,256]{4,1,3,2,0:T(4,128)(2,1)}, u32[]{:S(2)}, u32[]{:S(2)}) %all-to-all-start.2) | async-done | bytes 4194336 | tf_op jit(solution)/shard_map/all_to_all | solution.py:190
  527.6 4.3 all-to-all-start.3
  531.9 4.3 fusion.54
  536.2 5.0 multiply_convert_fusion
  541.6 3.5 copy.121
  557.9 5.1 shard_map.47
  563.0 4.9 shard_map.46
  568.9 4.8 shard_map.48
  574.7 51.1 %all-to-all-done.3 = bf16[32,4,2,32,256]{4,1,3,2,0:T(4,128)(2,1)} async-done(((bf16[32,4,2,32,256]{4,1,3,2,0:T(4,128)(2,1)}), bf16[32,4,2,32,256]{4,1,3,2,0:T(4,128)(2,1)}, u32[]{:S(2)}, u32[]{:S(2)}) %all-to-all-start.3) | async-done | bytes 4194336 | tf_op jit(solution)/shard_map/all_to_all | solution.py:190
  628.9 4.9 shard_map.49
  634.2 16.9 %all_to_all.25 = f32[4,256,256]{2,1,0:T(8,128)S(1)} all-to-all(f32[4,256,256]{2,1,0:T(8,128)S(1)} %add_add_fusion), channel_id=1, replica_groups=mesh['freq'=8,'dish'=4] {'dish'}, dimensions={0} | all-to-all | bytes 2097152 | tf_op jit(solution)/shard_map/all_to_all | solution.py:194
  (83 shorter events, 51.3 us)
Async XLA Ops:
  33.2 57.0 %copy-start.20 = (bf16[32,1,2,8192]{3,2,1,0:T(2,128)(2,1)S(1)}, bf16[32,1,2,8192]{3,2,1,0:T(2,128)(2,1)}, u32[]{:S(2)}) copy-start(bf16[32,1,2,8192]{3,2,1,0:T(2,128)(2,1)} %param.5) | copy-start | bytes 3145732
  33.2 57.8 %copy-start.23 = (s32[8]{0:T(128)S(1)}, s32[8]{0:T(128)}, u32[]{:S(2)}) copy-start(s32[8]{0:T(128)} %param.6) | copy-start | bytes 100
  101.8 10.3 %copy-start.16 = (bf16[32,2,4,64,128]{4,3,2,1,0:T(8,128)(2,1)S(1)}, bf16[32,2,4,64,128]{4,3,2,1,0:T(8,128)(2,1)}, u32[]{:S(2)}) copy-start(bf16[32,2,4,64,128]{4,3,2,1,0:T(8,128)(2,1)} %get-tuple-element.6) | copy-start | bytes 12582916
  101.8 11.3 %copy-start.17 = (bf16[32,2,4,64,128]{4,3,2,1,0:T(8,128)(2,1)S(1)}, bf16[32,2,4,64,128]{4,3,2,1,0:T(8,128)(2,1)}, u32[]{:S(2)}) copy-start(bf16[32,2,4,64,128]{4,3,2,1,0:T(8,128)(2,1)} %get-tuple-element.7) | copy-start | bytes 12582916
  101.8 12.5 %copy-start.18 = (bf16[32,2,4,64,128]{4,3,2,1,0:T(8,128)(2,1)S(1)}, bf16[32,2,4,64,128]{4,3,2,1,0:T(8,128)(2,1)}, u32[]{:S(2)}) copy-start(bf16[32,2,4,64,128]{4,3,2,1,0:T(8,128)(2,1)} %get-tuple-element.8) | copy-start | bytes 12582916
  101.9 13.7 %copy-start.19 = (bf16[32,2,4,64,128]{4,3,2,1,0:T(8,128)(2,1)S(1)}, bf16[32,2,4,64,128]{4,3,2,1,0:T(8,128)(2,1)}, u32[]{:S(2)}) copy-start(bf16[32,2,4,64,128]{4,3,2,1,0:T(8,128)(2,1)} %get-tuple-element.20) | copy-start | bytes 12582916
  101.9 13.7 %copy-start.21 = (f32[1,8192]{1,0:T(1,128)S(1)}, f32[1,8192]{1,0:T(1,128)}, u32[]{:S(2)}) copy-start(f32[1,8192]{1,0:T(1,128)} %get-tuple-element.50) | copy-start | bytes 98308
  115.6 6.4 copy-start.14
  115.6 6.4 copy-start.15
  121.9 8.7 %copy-start.10 = (bf16[32,2,4,64,128]{4,3,2,1,0:T(8,128)(2,1)S(1)}, bf16[32,2,4,64,128]{4,3,2,1,0:T(8,128)(2,1)}, u32[]{:S(2)}) copy-start(bf16[32,2,4,64,128]{4,3,2,1,0:T(8,128)(2,1)} %get-tuple-element.5) | copy-start | bytes 12582916
  121.9 8.7 %copy-start.11 = (bf16[32,2,4,64,128]{4,3,2,1,0:T(8,128)(2,1)S(1)}, bf16[32,2,4,64,128]{4,3,2,1,0:T(8,128)(2,1)}, u32[]{:S(2)}) copy-start(bf16[32,2,4,64,128]{4,3,2,1,0:T(8,128)(2,1)} %get-tuple-element.13) | copy-start | bytes 12582916
  121.9 10.1 %copy-start.12 = (bf16[32,2,4,64,128]{4,3,2,1,0:T(8,128)(2,1)S(1)}, bf16[32,2,4,64,128]{4,3,2,1,0:T(8,128)(2,1)}, u32[]{:S(2)}) copy-start(bf16[32,2,4,64,128]{4,3,2,1,0:T(8,128)(2,1)} %get-tuple-element.14) | copy-start | bytes 12582916
  122.0 11.3 %copy-start.13 = (bf16[32,2,4,64,128]{4,3,2,1,0:T(8,128)(2,1)S(1)}, bf16[32,2,4,64,128]{4,3,2,1,0:T(8,128)(2,1)}, u32[]{:S(2)}) copy-start(bf16[32,2,4,64,128]{4,3,2,1,0:T(8,128)(2,1)} %get-tuple-element.15) | copy-start | bytes 12582916
  158.8 6.9 %copy-start.7 = (bf16[32,4,1,64,128]{4,3,1,0,2:T(8,128)(2,1)S(1)}, bf16[32,4,1,64,128]{4,3,1,0,2:T(8,128)(2,1)}, u32[]{:S(2)}) copy-start(bf16[32,4,1,64,128]{4,3,1,0,2:T(8,128)(2,1)} %get-tuple-element.53) | copy-start | bytes 6291460
  158.8 6.9 %copy-start.8 = (bf16[32,4,1,64,128]{4,3,1,0,2:T(8,128)(2,1)S(1)}, bf16[32,4,1,64,128]{4,3,1,0,2:T(8,128)(2,1)}, u32[]{:S(2)}) copy-start(bf16[32,4,1,64,128]{4,3,1,0,2:T(8,128)(2,1)} %get-tuple-element.54) | copy-start | bytes 6291460
  165.8 4.5 copy-start.5
  165.8 4.5 copy-start.6
  170.3 4.5 copy-start.4
  229.9 101.3 %all-to-all-start.1 = ((bf16[32,4,2,32,256]{4,1,3,2,0:T(4,128)(2,1)}), bf16[32,4,2,32,256]{4,1,3,2,0:T(4,128)(2,1)}, u32[]{:S(2)}, u32[]{:S(2)}) async-start(bf16[32,4,2,32,256]{4,1,3,2,0:T(4,128)(2,1)} %copy.130), calls=%async_computation.1 | async-start | bytes 8388608 | tf_op jit(solution)/shard_map/all_to_all | solution.py:190
  331.2 98.4 %all-to-all-start = ((bf16[32,4,2,32,256]{4,1,3,2,0:T(4,128)(2,1)}), bf16[32,4,2,32,256]{4,1,3,2,0:T(4,128)(2,1)}, u32[]{:S(2)}, u32[]{:S(2)}) async-start(bf16[32,4,2,32,256]{4,1,3,2,0:T(4,128)(2,1)} %copy.119), calls=%async_computation | async-start | bytes 8388608 | tf_op jit(solution)/shard_map/all_to_all | solution.py:190
  429.6 97.9 %all-to-all-start.2 = ((bf16[32,4,2,32,256]{4,1,3,2,0:T(4,128)(2,1)}), bf16[32,4,2,32,256]{4,1,3,2,0:T(4,128)(2,1)}, u32[]{:S(2)}, u32[]{:S(2)}) async-start(bf16[32,4,2,32,256]{4,1,3,2,0:T(4,128)(2,1)} %copy.139), calls=%async_computation.2 | async-start | bytes 8388608 | tf_op jit(solution)/shard_map/all_to_all | solution.py:190
  448.2 6.7 %copy-start.9 = (bf16[32,4,1,32,256]{4,3,1,0,2:T(8,128)(2,1)S(1)}, bf16[32,4,1,32,256]{4,3,1,0,2:T(8,128)(2,1)}, u32[]{:S(2)}) copy-start(bf16[32,4,1,32,256]{4,3,1,0,2:T(8,128)(2,1)} %stack.151) | copy-start | bytes 6291460
  462.1 69.7 %copy-start.22 = (s32[4,256]{1,0:T(4,128)S(1)}, s32[4,256]{1,0:T(4,128)}, u32[]{:S(2)}) copy-start(s32[4,256]{1,0:T(4,128)} %param.7) | copy-start | bytes 12292
  527.6 98.2 %all-to-all-start.3 = ((bf16[32,4,2,32,256]{4,1,3,2,0:T(4,128)(2,1)}), bf16[32,4,2,32,256]{4,1,3,2,0:T(4,128)(2,1)}, u32[]{:S(2)}, u32[]{:S(2)}) async-start(bf16[32,4,2,32,256]{4,1,3,2,0:T(4,128)(2,1)} %copy.148), calls=%async_computation.3 | async-start | bytes 8388608 | tf_op jit(solution)/shard_map/all_to_all | solution.py:190
  567.9 1.0 copy-start
  573.7 1.0 copy-start.2
  628.9 4.9 copy-start.1
  628.9 4.9 copy-start.3

commit v2 on v1

v2 whole, which is shorter than its diff:
```python
import math

import jax
import jax.numpy as jnp
from jax import lax
from jax.experimental import pallas as pl
from jax.experimental.pallas import tpu as pltpu
from jax.sharding import PartitionSpec as P

NCHAN = 8192
CHA = 64
CHB = 128
TAPS = 4
FRAMES = 16
N_DISH = 4
CHUNKS = 4


full_turn = 2.0 * math.pi


def fourier_table(row_index, col_index, modulus, scaling):
    phases = row_index[:, None] * col_index[None, :] % modulus
    angles = full_turn / modulus * phases.astype(jnp.float32)
    cosine_table = (jnp.cos(angles) * scaling).astype(jnp.bfloat16)
    sine_table = (jnp.sin(angles) * scaling).astype(jnp.bfloat16)
    upper_rows = jnp.stack([cosine_table, -sine_table], axis=1)
    lower_rows = jnp.stack([sine_table, cosine_table], axis=1)
    return jnp.stack([upper_rows, lower_rows], axis=0)


def filter_window():
    sample_index = jnp.arange(TAPS * NCHAN, dtype=jnp.float32)
    centred = (sample_index - TAPS * NCHAN / 2 + 0.5) / NCHAN
    taper_curve = 0.5 - 0.5 * jnp.cos(full_turn * (sample_index + 0.5) / (TAPS * NCHAN))
    shaped_window = (jnp.sinc(centred) * taper_curve).reshape(TAPS, NCHAN)
    energy = jnp.mean(jnp.sum(shaped_window * shaped_window, axis=0))
    return shaped_window / jnp.sqrt(energy)


def channel_kernel(start, frames, v_ref, window_ref, first_ref, turn_ref, second_ref, gain_ref, out_ref):
    rows = []
    for f in range(frames):
        filtered = window_ref[0] * v_ref[0, start + f].astype(jnp.float32)
        for t in range(1, TAPS):
            filtered = filtered + window_ref[t] * v_ref[0, start + f + t].astype(jnp.float32)
        section = jnp.dot(
            first_ref[...], filtered.astype(jnp.bfloat16), preferred_element_type=jnp.float32
        )
        real, imag = section[:CHA], section[CHA:]
        cosine, sine = turn_ref[0], turn_ref[1]
        turned = jnp.concatenate(
            [real * cosine - imag * sine, real * sine + imag * cosine], axis=1
        )
        rows.append(turned.astype(jnp.bfloat16))
    spectrum = lax.dot_general(
        second_ref[...],
        jnp.concatenate(rows, axis=0),
        (((1,), (1,)), ((), ())),
        preferred_element_type=jnp.float32,
    )
    real, imag = spectrum[:CHB], spectrum[CHB:]
    gain_real = gain_ref[0, 0].astype(jnp.float32)
    gain_imag = gain_ref[0, 1].astype(jnp.float32)
    out_ref[0, 0] = (real * gain_real - imag * gain_imag).astype(jnp.bfloat16)
    out_ref[0, 1] = (real * gain_imag + imag * gain_real).astype(jnp.bfloat16)


def channelize(start, frames, volts, window, first_table, turn, second_table, gains):
    feeds = volts.shape[0]
    width = frames * CHA

    def whole(array):
        return pl.BlockSpec(array.shape, lambda r: (0,) * array.ndim)

    def own(array):
        return pl.BlockSpec((1,) + array.shape[1:], lambda r: (r,) + (0,) * (array.ndim - 1))

    out = jax.ShapeDtypeStruct((feeds, 2, CHB, width), jnp.bfloat16)
    return pl.pallas_call(
        lambda *refs: channel_kernel(start, frames, *refs),
        grid=(feeds,),
        in_specs=[
            own(volts),
            whole(window),
            whole(first_table),
            whole(turn),
            whole(second_table),
            own(gains),
        ],
        out_specs=own(out),
        out_shape=out,
        compiler_params=pltpu.CompilerParams(vmem_limit_bytes=32 * 2**20),
        cost_estimate=pl.CostEstimate(
            flops=feeds * frames * (2 * 128**3 + 2 * 64 * 256 * 256),
            bytes_accessed=volts.size * 2 + gains.size * 2 + feeds * 512 * width,
            transcendentals=0,
        ),
    )(volts, window, first_table, turn, second_table, gains)


def beam_kernel(scale, x_ref, table_ref, twist_ref, power_ref):
    groups, _, _, _, rows, width = x_ref.shape
    frames = width // CHA
    positions = twist_ref.shape[2]
    parts = []
    for d in range(N_DISH):
        sums = None
        for p in range(2):
            feeds = x_ref[:, d, p, 0]
            if rows % 16:
                feeds = feeds.astype(jnp.float32).reshape(groups * rows, width).astype(jnp.bfloat16)
            else:
                feeds = feeds.reshape(groups * rows, width)
            term = lax.dot_general(
                feeds,
                table_ref[d, p],
                (((0,), (0,)), ((), ())),
                preferred_element_type=jnp.float32,
            )
            sums = term if sums is None else sums + term
        real, imag = sums[:, :positions], sums[:, positions:]
        cosine, sine = twist_ref[d, 0:1], twist_ref[d, 1:2]
        parts.append(
            (
                (real * cosine - imag * sine).astype(jnp.bfloat16).astype(jnp.float32),
                (real * sine + imag * cosine).astype(jnp.bfloat16).astype(jnp.float32),
            )
        )
    (r0, i0), (r1, i1), (r2, i2), (r3, i3) = parts
    ar, ai, br, bi = r0 + r2, i0 + i2, r1 + r3, i1 + i3
    cr, ci, dr, di = r0 - r2, i0 - i2, r1 - r3, i1 - i3
    beams = (
        (ar + br, ai + bi),
        (ar - br, ai - bi),
        (cr + di, ci - dr),
        (cr - di, ci + dr),
    )

    for s, (real, imag) in enumerate(beams):
        power = (real * real + imag * imag) * scale
        power_ref[s] = sum(power[f * CHA : (f + 1) * CHA] for f in range(frames))


def beam_power(gathered, tables, twist):
    groups, dishes, _, parts, rows, width = gathered.shape
    positions = twist.shape[2]
    return pl.pallas_call(
        lambda *refs: beam_kernel(1.0 / (N_DISH * FRAMES), *refs),
        grid=(parts,),
        in_specs=[
            pl.BlockSpec((groups, dishes, 2, 1, rows, width), lambda e: (0, 0, 0, e, 0, 0)),
            pl.BlockSpec(tables.shape, lambda e: (0, 0, 0, 0)),
            pl.BlockSpec(twist.shape, lambda e: (0, 0, 0)),
        ],
        out_specs=pl.BlockSpec((N_DISH, CHA, positions), lambda e: (0, e, 0)),
        out_shape=jax.ShapeDtypeStruct((N_DISH, parts * CHA, positions), jnp.float32),
        compiler_params=pltpu.CompilerParams(vmem_limit_bytes=40 * 2**20),
        cost_estimate=pl.CostEstimate(
            flops=parts * dishes * groups * rows * 2 * width * positions * 4,
            bytes_accessed=gathered.size * 2 + tables.size * 2,
            transcendentals=0,
        ),
    )(gathered, tables, twist)


def body(voltages, feed_gains, block_assign, grid_rows):
    dish_rows = voltages.shape[0]
    block_count = lax.axis_size("freq")
    dish_count = lax.axis_size("dish")
    devices = block_count * dish_count
    block_width = NCHAN // block_count
    parts = CHB // devices
    grid_len = grid_rows.shape[1]
    total_dishes = grid_len * dish_count

    step = FRAMES // CHUNKS
    window = jnp.repeat(filter_window().reshape(TAPS, CHA, CHB), 2, axis=1)
    first_index = jnp.arange(CHA, dtype=jnp.int32)
    second_index = jnp.arange(CHB, dtype=jnp.int32)
    first_table = fourier_table(first_index, first_index, CHA, 1.0 / math.sqrt(CHA))
    first_table = jnp.transpose(first_table, (2, 3, 1, 0)).reshape(2 * CHA, 2 * CHA)
    turn_angles = -(full_turn / NCHAN) * (
        first_index[:, None] * second_index[None, :] % NCHAN
    ).astype(jnp.float32)
    turn = jnp.stack([jnp.cos(turn_angles), jnp.sin(turn_angles)])
    per_block = CHB // block_count
    ordered = (
        block_assign[:, None] * per_block + jnp.arange(per_block, dtype=jnp.int32)[None]
    ).reshape(CHB)
    second_table = fourier_table(second_index, ordered, CHB, 1.0 / math.sqrt(CHB))
    second_table = jnp.transpose(second_table, (2, 3, 0, 1)).reshape(2 * CHB, 2 * CHB)
    chosen = (jnp.arange(block_count)[:, None] == block_assign[None, :]).astype(jnp.bfloat16)
    gains = jnp.einsum(
        "rpbw,bn->rpnw",
        feed_gains[:, 0].reshape(dish_rows, 2, block_count, block_width),
        chosen,
        preferred_element_type=jnp.float32,
    ).reshape(dish_rows, 2, CHB, CHA)
    gains = jnp.tile(gains.astype(jnp.bfloat16), (1, 1, 1, step))

    positions = jnp.arange(grid_len, dtype=jnp.int32)
    tables = jax.vmap(
        lambda line: fourier_table(line, positions, grid_len, 1.0 / math.sqrt(grid_len))
    )(grid_rows).reshape(dish_count, 2, grid_len, 2 * grid_len)
    classes = jnp.arange(dish_count, dtype=jnp.int32)
    twist_angles = -(full_turn / total_dishes) * (
        classes[:, None] * positions[None, :] % total_dishes
    ).astype(jnp.float32)
    twist = jnp.stack([jnp.cos(twist_angles), jnp.sin(twist_angles)], axis=1)

    spans = FRAMES + TAPS - 1
    volts = voltages[:, 0].reshape(dish_rows, 2, spans * CHA, CHB)
    volts = jnp.transpose(volts, (0, 2, 1, 3)).reshape(dish_rows, spans, 2 * CHA, CHB)
    total = None
    for chunk in range(CHUNKS):
        spectra = channelize(
            chunk * step, step, volts, window, first_table, turn, second_table, gains
        )
        spectra = spectra.reshape(dish_rows, 2, devices, parts, step * CHA)
        sent = jnp.transpose(spectra, (2, 1, 3, 0, 4))
        sent, first_table = lax.optimization_barrier((sent, first_table))
        gathered = lax.all_to_all(sent, ("freq", "dish"), split_axis=0, concat_axis=0, tiled=True)
        gathered = gathered.reshape(block_count, dish_count, 2, parts, dish_rows, step * CHA)
        power = beam_power(gathered, tables, twist)
        total = power if total is None else total + power
    out = lax.all_to_all(total, "dish", split_axis=0, concat_axis=0, tiled=True)
    return out.reshape(block_width, grid_len)


def solution(mesh):
    placed = (P("freq", "dish", None, None), P("freq", "dish", None, None), P(), P())
    return jax.shard_map(
        body, mesh=mesh, in_specs=placed, out_specs=P("freq", "dish"), check_vma=False
    )
```

time: 663 us -> 506 us (0.76)
  local copies, waits for them, and re-layouts: 235 us -> 107 us
  Pallas kernels: 19.6 us -> 123 us
  matrix products: 52.4 us -> 2.12 us
  other arithmetic: 63.5 us -> 13.8 us
  waiting for transfers between devices: 243 us -> 205 us
  starting transfers between devices: 20.2 us -> 30.3 us
    another operation x17 -> x2, local copies, waits for them, and re-layouts: 120 us -> 10.7 us  [body(): gains = jnp.tile(gains.astype(jnp.bfloat16), (1, 1, 1, step))]
    pallas_call x0 -> x4, Pallas kernels: none -> 99.6 us  [channelize(): pl.pallas_call(lambda *refs: channel_kernel(start, frames, *refs), grid=(...]
    reshape x1 -> x10, local copies, waits for them, and re-layouts: 2.57 us -> 62.7 us  [the longest x8 62.5 us: body(): spectra = spectra.reshape(dish_rows, 2, devices, parts, step * CHA)]
    slice x2 -> x0, local copies, waits for them, and re-layouts: 55 us -> none  [channelize(): filtered = window[0] * framed[:, :, 0:frames]]
    dot_general x8 -> x0, matrix products: 51.9 us -> none  [the longest x4 31.4 us: channelize(): jnp.einsum('rpfab,paqc->rfqcb', filtered, first_table, preferred_element_...]
    another operation x2 -> x1, other arithmetic: 39.2 us -> 0.01 us  [body(): turn = jnp.stack([jnp.cos(turn_angles), jnp.sin(turn_angles)])]
    all_to_all x4, waiting for transfers between devices: 243 us -> 205 us  [body(): lax.all_to_all(sent, ('freq', 'dish'), split_axis=0, concat_axis=0, tiled...]
    transpose x4 -> x2, local copies, waits for them, and re-layouts: 20.9 us -> 0.2 us  [the longest x1 0.13 us: body(): jnp.transpose(second_table, (2, 3, 0, 1)).reshape(2 * CHB, 2 * CHB)]
  transfers between devices with their start and end apart: 4 -> 4, of which waited for: 4 -> 4; matrix products, arithmetic and copies ran while one was open for 18% -> 13% of each run, Pallas kernels for 2% -> 18%
where the time goes in v2:
time: 506 us; the launch traced here: 499 us
  waiting for transfers between devices  205 us (41%)
  Pallas kernels  123 us (24%)
  local copies, waits for them, and re-layouts  107 us (21%)
  starting transfers between devices  30.3 us (6%)
  blocking collectives  16.9 us (3%)
  other arithmetic  13.8 us (3%)
    all_to_all x4, waiting for transfers between devices, body(): lax.all_to_all(sent, ('freq', 'dish'), split_axis=0, concat_axis=0, tiled...  205 us
    pallas_call x4, Pallas kernels, channelize(): pl.pallas_call(lambda *refs: channel_kernel(start, frames, *refs), grid=(...  99.6 us
    reshape x8, local copies, waits for them, and re-layouts, body(): spectra = spectra.reshape(dish_rows, 2, devices, parts, step * CHA)  62.5 us
    all_to_all x4, starting transfers between devices, body(): lax.all_to_all(sent, ('freq', 'dish'), split_axis=0, concat_axis=0, tiled...  30.3 us
    pallas_call x4, Pallas kernels, beam_power(): pl.pallas_call(lambda *refs: beam_kernel(1.0 / (N_DISH * FRAMES), *refs),...  23.5 us
    unnamed x28, local copies, waits for them, and re-layouts  19.6 us
    all_to_all x1, blocking collectives, body(): out = lax.all_to_all(total, 'dish', split_axis=0, concat_axis=0, tiled=True)  16.9 us
    another operation x2, local copies, waits for them, and re-layouts, body(): gains = jnp.tile(gains.astype(jnp.bfloat16), (1, 1, 1, step))  10.7 us
  transfers between devices with their start and end apart: 4, of which 4 were waited for; matrix products, arithmetic and copies ran while one was open for 13% of the time, Pallas kernels for 18%

profile of v2, /device:TPU:0, one launch (start us, length us, event | category | flops | bytes accessed | tf_op | source)
XLA Modules:
  0.0 499.2 jit_solution(11518275952069455794)
XLA Ops:
  0.0 1.2 fusion.30
  1.5 0.7 broadcast_multiply_fusion
  4.9 1.8 reshape_squeeze.7
  6.8 2.1 fusion
  8.9 2.9 convert_element_type.196
  11.9 1.6 copy.33
  13.5 4.2 tile.4
  17.7 6.5 %copy.35.refs_5_ = bf16[32,2,128,256]{3,2,1,0:T(8,128)(2,1)} copy(bf16[32,2,128,256]{2,3,1,0:T(8,128)(2,1)} %bitcast.79) | data formatting | bytes 8388608 | tf_op jit(solution)/shard_map/tile | solution.py:200
  24.3 2.2 copy-done
  26.5 24.9 %shard_map.46 = bf16[32,2,128,256]{3,2,1,0:T(8,128)(2,1)S(1)} custom-call(bf16[32,19,128,128]{3,2,1,0:T(8,128)(2,1)} %bitcast.75, f32[4,128,128]{2,1,0:T(8,128)S(1)} %bitcast.67, bf16[128,128]{1,0:T(8,128)(2,1)S(1)} %copy.34.refs_2_, f32[2,64,128]{2,1,0:T(8,128)S(1)} %pad_maximum_fusion.refs_3_, bf16[256,256]{1,0:T(8,128)(2,1)S(1)} %bitcast.71, ...), custom_call_target="tpu_custom_call" | custom-call | flops 1610612736 | bytes 28311552 | tf_op jit(solution)/shard_map/pallas_call | solution.py:80
  51.4 2.0 copy-done.5
  53.4 6.9 %reshape.496 = bf16[32,2,32,4,256]{4,3,2,1,0:T(4,128)(2,1)} reshape(bf16[32,2,128,256]{3,2,1,0:T(8,128)(2,1)} %copy-done.5) | data formatting | bytes 8388608 | tf_op jit(solution)/shard_map/reshape | solution.py:220
  60.3 8.7 %copy.63 = bf16[32,2,32,4,256]{4,0,3,1,2:T(8,128)(2,1)} copy(bf16[32,2,32,4,256]{4,3,2,1,0:T(4,128)(2,1)} %reshape.496) | data formatting | bytes 8388608 | tf_op jit(solution)/shard_map/reshape | solution.py:220
  69.0 7.7 %all-to-all-start = ((bf16[32,2,4,32,256]{4,3,2,1,0:T(8,128)(2,1)}), bf16[32,2,4,32,256]{4,3,2,1,0:T(8,128)(2,1)}, u32[]{:S(2)}, u32[]{:S(2)}) async-start(bf16[32,2,4,32,256]{4,3,2,1,0:T(8,128)(2,1)} %bitcast.83), calls=%async_computation | async-start | bytes 8388608 | tf_op jit(solution)/shard_map/all_to_all | solution.py:223
  76.8 2.2 copy-done.1
  79.0 24.9 %shard_map.48 = bf16[32,2,128,256]{3,2,1,0:T(8,128)(2,1)S(1)} custom-call(bf16[32,19,128,128]{3,2,1,0:T(8,128)(2,1)} %bitcast.76, f32[4,128,128]{2,1,0:T(8,128)S(1)} %bitcast.68, bf16[128,128]{1,0:T(8,128)(2,1)S(1)} %copy.39.refs_2_, f32[2,64,128]{2,1,0:T(8,128)S(1)} %pad_maximum_fusion.refs_3_, bf16[256,256]{1,0:T(8,128)(2,1)S(1)} %bitcast.72, ...), custom_call_target="tpu_custom_call" | custom-call | flops 1610612736 | bytes 28311552 | tf_op jit(solution)/shard_map/pallas_call | solution.py:80
  103.9 1.9 copy-done.6
  105.9 6.9 %reshape.499 = bf16[32,2,32,4,256]{4,3,2,1,0:T(4,128)(2,1)} reshape(bf16[32,2,128,256]{3,2,1,0:T(8,128)(2,1)} %copy-done.6) | data formatting | bytes 8388608 | tf_op jit(solution)/shard_map/reshape | solution.py:220
  112.8 8.7 %copy.62 = bf16[32,2,32,4,256]{4,0,3,1,2:T(8,128)(2,1)} copy(bf16[32,2,32,4,256]{4,3,2,1,0:T(4,128)(2,1)} %reshape.499) | data formatting | bytes 8388608 | tf_op jit(solution)/shard_map/reshape | solution.py:220
  121.4 49.2 %all-to-all-done = bf16[32,2,4,32,256]{4,3,2,1,0:T(8,128)(2,1)} async-done(((bf16[32,2,4,32,256]{4,3,2,1,0:T(8,128)(2,1)}), bf16[32,2,4,32,256]{4,3,2,1,0:T(8,128)(2,1)}, u32[]{:S(2)}, u32[]{:S(2)}) %all-to-all-start) | async-done | bytes 4194336 | tf_op jit(solution)/shard_map/all_to_all | solution.py:223
  170.6 4.0 all-to-all-start.1
  174.8 2.2 copy-done.2
  177.0 24.9 %shard_map.50 = bf16[32,2,128,256]{3,2,1,0:T(8,128)(2,1)S(1)} custom-call(bf16[32,19,128,128]{3,2,1,0:T(8,128)(2,1)} %bitcast.77, f32[4,128,128]{2,1,0:T(8,128)S(1)} %bitcast.69, bf16[128,128]{1,0:T(8,128)(2,1)S(1)} %copy.42.refs_2_, f32[2,64,128]{2,1,0:T(8,128)S(1)} %pad_maximum_fusion.refs_3_, bf16[256,256]{1,0:T(8,128)(2,1)S(1)} %bitcast.73, ...), custom_call_target="tpu_custom_call" | custom-call | flops 1610612736 | bytes 28311552 | tf_op jit(solution)/shard_map/pallas_call | solution.py:80
  201.9 1.9 copy-done.7
  203.8 7.0 %reshape.501 = bf16[32,2,32,4,256]{4,3,2,1,0:T(4,128)(2,1)} reshape(bf16[32,2,128,256]{3,2,1,0:T(8,128)(2,1)} %copy-done.7) | data formatting | bytes 8388608 | tf_op jit(solution)/shard_map/reshape | solution.py:220
  210.8 8.7 %copy.61 = bf16[32,2,32,4,256]{4,0,3,1,2:T(8,128)(2,1)} copy(bf16[32,2,32,4,256]{4,3,2,1,0:T(4,128)(2,1)} %reshape.501) | data formatting | bytes 8388608 | tf_op jit(solution)/shard_map/reshape | solution.py:220
  219.5 49.1 %all-to-all-done.1 = bf16[32,2,4,32,256]{4,3,2,1,0:T(8,128)(2,1)} async-done(((bf16[32,2,4,32,256]{4,3,2,1,0:T(8,128)(2,1)}), bf16[32,2,4,32,256]{4,3,2,1,0:T(8,128)(2,1)}, u32[]{:S(2)}, u32[]{:S(2)}) %all-to-all-start.1) | async-done | bytes 4194336 | tf_op jit(solution)/shard_map/all_to_all | solution.py:223
  268.5 14.8 %all-to-all-start.2 = ((bf16[32,2,4,32,256]{4,3,2,1,0:T(8,128)(2,1)}), bf16[32,2,4,32,256]{4,3,2,1,0:T(8,128)(2,1)}, u32[]{:S(2)}, u32[]{:S(2)}) async-start(bf16[32,2,4,32,256]{4,3,2,1,0:T(8,128)(2,1)} %bitcast.81), calls=%async_computation.2 | async-start | bytes 8388608 | tf_op jit(solution)/shard_map/all_to_all | solution.py:223
  283.4 2.2 copy-done.3
  285.6 24.9 %shard_map.52 = bf16[32,2,128,256]{3,2,1,0:T(8,128)(2,1)S(1)} custom-call(bf16[32,19,128,128]{3,2,1,0:T(8,128)(2,1)} %bitcast.78, f32[4,128,128]{2,1,0:T(8,128)S(1)} %bitcast.70, bf16[128,128]{1,0:T(8,128)(2,1)S(1)} %copy.45.refs_2_, f32[2,64,128]{2,1,0:T(8,128)S(1)} %pad_maximum_fusion.refs_3_, bf16[256,256]{1,0:T(8,128)(2,1)S(1)} %bitcast.74, ...), custom_call_target="tpu_custom_call" | custom-call | flops 1610612736 | bytes 28311552 | tf_op jit(solution)/shard_map/pallas_call | solution.py:80
  310.5 2.0 copy-done.4
  312.6 7.0 %reshape.503 = bf16[32,2,32,4,256]{4,3,2,1,0:T(4,128)(2,1)} reshape(bf16[32,2,128,256]{3,2,1,0:T(8,128)(2,1)} %copy-done.4) | data formatting | bytes 8388608 | tf_op jit(solution)/shard_map/reshape | solution.py:220
  319.5 8.8 %copy.60 = bf16[32,2,32,4,256]{4,0,3,1,2:T(8,128)(2,1)} copy(bf16[32,2,32,4,256]{4,3,2,1,0:T(4,128)(2,1)} %reshape.503) | data formatting | bytes 8388608 | tf_op jit(solution)/shard_map/reshape | solution.py:220
  328.3 48.9 %all-to-all-done.2 = bf16[32,2,4,32,256]{4,3,2,1,0:T(8,128)(2,1)} async-done(((bf16[32,2,4,32,256]{4,3,2,1,0:T(8,128)(2,1)}), bf16[32,2,4,32,256]{4,3,2,1,0:T(8,128)(2,1)}, u32[]{:S(2)}, u32[]{:S(2)}) %all-to-all-start.2) | async-done | bytes 4194336 | tf_op jit(solution)/shard_map/all_to_all | solution.py:223
  377.2 3.8 all-to-all-start.3
  381.1 4.3 fusion.7
  385.4 5.0 %multiply_convert_fusion = (bf16[4,256,1,256]{3,1,2,0:T(8,128)(2,1)S(1)}, bf16[4,256,1,256]{3,1,2,0:T(8,128)(2,1)S(1)}) fusion(s32[4,256]{1,0:T(4,128)S(1)} %copy-done.12), kind=kLoop, calls=%fused_computation.16 | loop fusion | flops 4718592 | bytes 1052672 | tf_op jit(solution)/shard_map/vmap()/convert_element_type | solution.py:26
  390.8 3.5 copy.37
  394.3 3.2 reshape.498.refs_1_
  397.6 5.8 %shard_map.47 = f32[4,256,256]{2,1,0:T(8,128)S(1)} custom-call(bf16[8,4,2,4,32,256]{5,4,3,2,1,0:T(8,128)(2,1)} %bitcast.15.refs_0_, bf16[4,2,256,512]{3,2,1,0:T(8,128)(2,1)S(1)} %reshape.498.refs_1_, f32[4,2,256]{2,1,0:T(2,128)S(1)} %pad_maximum_fusion.1.refs_2_), custom_call_target="tpu_custom_call" | custom-call | flops 2147483648 | bytes 6291456 | tf_op jit(solution)/shard_map/pallas_call | solution.py:148
  403.5 5.8 %shard_map.49 = f32[4,256,256]{2,1,0:T(8,128)S(1)} custom-call(bf16[8,4,2,4,32,256]{5,4,3,2,1,0:T(8,128)(2,1)} %bitcast.22.refs_0_, bf16[4,2,256,512]{3,2,1,0:T(8,128)(2,1)S(1)} %reshape.498.refs_1_, f32[4,2,256]{2,1,0:T(2,128)S(1)} %pad_maximum_fusion.1.refs_2_), custom_call_target="tpu_custom_call" | custom-call | flops 2147483648 | bytes 6291456 | tf_op jit(solution)/shard_map/pallas_call | solution.py:148
  409.3 1.0 copy-done.8
  410.4 5.8 %shard_map.51 = f32[4,256,256]{2,1,0:T(8,128)S(1)} custom-call(bf16[8,4,2,4,32,256]{5,4,3,2,1,0:T(8,128)(2,1)} %bitcast.24.refs_0_, bf16[4,2,256,512]{3,2,1,0:T(8,128)(2,1)S(1)} %reshape.498.refs_1_, f32[4,2,256]{2,1,0:T(2,128)S(1)} %pad_maximum_fusion.1.refs_2_), custom_call_target="tpu_custom_call" | custom-call | flops 2147483648 | bytes 6291456 | tf_op jit(solution)/shard_map/pallas_call | solution.py:148
  416.2 1.0 copy-done.10
  417.2 57.8 %all-to-all-done.3 = bf16[32,2,4,32,256]{4,3,2,1,0:T(8,128)(2,1)} async-done(((bf16[32,2,4,32,256]{4,3,2,1,0:T(8,128)(2,1)}), bf16[32,2,4,32,256]{4,3,2,1,0:T(8,128)(2,1)}, u32[]{:S(2)}, u32[]{:S(2)}) %all-to-all-start.3) | async-done | bytes 4194336 | tf_op jit(solution)/shard_map/all_to_all | solution.py:223
  474.9 6.0 %shard_map.53 = f32[4,256,256]{2,1,0:T(8,128)S(1)} custom-call(bf16[8,4,2,4,32,256]{5,4,3,2,1,0:T(8,128)(2,1)} %bitcast.26.refs_0_, bf16[4,2,256,512]{3,2,1,0:T(8,128)(2,1)S(1)} %reshape.498.refs_1_, f32[4,2,256]{2,1,0:T(2,128)S(1)} %pad_maximum_fusion.1.refs_2_), custom_call_target="tpu_custom_call" | custom-call | flops 2147483648 | bytes 6291456 | tf_op jit(solution)/shard_map/pallas_call | solution.py:148
  481.2 16.9 %all_to_all.25 = f32[4,256,256]{2,1,0:T(8,128)S(1)} all-to-all(f32[4,256,256]{2,1,0:T(8,128)S(1)} %add_add_fusion), channel_id=1, replica_groups=mesh['freq'=8,'dish'=4] {'dish'}, dimensions={0} | all-to-all | bytes 2097152 | tf_op jit(solution)/shard_map/all_to_all | solution.py:227
  498.1 1.0 copy.66
  (44 shorter events, 3.5 us)
Async XLA Ops:
  24.3 2.2 copy-start
  51.4 2.0 copy-start.5
  69.0 101.6 %all-to-all-start = ((bf16[32,2,4,32,256]{4,3,2,1,0:T(8,128)(2,1)}), bf16[32,2,4,32,256]{4,3,2,1,0:T(8,128)(2,1)}, u32[]{:S(2)}, u32[]{:S(2)}) async-start(bf16[32,2,4,32,256]{4,3,2,1,0:T(8,128)(2,1)} %bitcast.83), calls=%async_computation | async-start | bytes 8388608 | tf_op jit(solution)/shard_map/all_to_all | solution.py:223
  76.8 2.2 copy-start.1
  103.9 1.9 copy-start.6
  170.6 97.9 %all-to-all-start.1 = ((bf16[32,2,4,32,256]{4,3,2,1,0:T(8,128)(2,1)}), bf16[32,2,4,32,256]{4,3,2,1,0:T(8,128)(2,1)}, u32[]{:S(2)}, u32[]{:S(2)}) async-start(bf16[32,2,4,32,256]{4,3,2,1,0:T(8,128)(2,1)} %bitcast.82), calls=%async_computation.1 | async-start | bytes 8388608 | tf_op jit(solution)/shard_map/all_to_all | solution.py:223
  174.8 2.2 copy-start.2
  201.9 1.9 copy-start.7
  268.5 108.7 %all-to-all-start.2 = ((bf16[32,2,4,32,256]{4,3,2,1,0:T(8,128)(2,1)}), bf16[32,2,4,32,256]{4,3,2,1,0:T(8,128)(2,1)}, u32[]{:S(2)}, u32[]{:S(2)}) async-start(bf16[32,2,4,32,256]{4,3,2,1,0:T(8,128)(2,1)} %bitcast.81), calls=%async_computation.2 | async-start | bytes 8388608 | tf_op jit(solution)/shard_map/all_to_all | solution.py:223
  283.4 2.2 copy-start.3
  310.5 2.0 copy-start.4
  328.3 52.8 %copy-start.12 = (s32[4,256]{1,0:T(4,128)S(1)}, s32[4,256]{1,0:T(4,128)}, u32[]{:S(2)}) copy-start(s32[4,256]{1,0:T(4,128)} %param.7) | copy-start | bytes 12292
  377.2 97.7 %all-to-all-start.3 = ((bf16[32,2,4,32,256]{4,3,2,1,0:T(8,128)(2,1)}), bf16[32,2,4,32,256]{4,3,2,1,0:T(8,128)(2,1)}, u32[]{:S(2)}, u32[]{:S(2)}) async-start(bf16[32,2,4,32,256]{4,3,2,1,0:T(8,128)(2,1)} %bitcast.80), calls=%async_computation.3 | async-start | bytes 8388608 | tf_op jit(solution)/shard_map/all_to_all | solution.py:223
  409.3 1.0 copy-start.8
  416.2 1.0 copy-start.10
  474.9 6.0 %copy-start.9 = (f32[4,256,256]{2,1,0:T(8,128)S(1)}, f32[4,256,256]{2,1,0:T(8,128)}, u32[]{:S(2)}) copy-start(f32[4,256,256]{2,1,0:T(8,128)} %copy-done.8) | copy-start | bytes 3145732
  474.9 6.0 %copy-start.11 = (f32[4,256,256]{2,1,0:T(8,128)S(1)}, f32[4,256,256]{2,1,0:T(8,128)}, u32[]{:S(2)}) copy-start(f32[4,256,256]{2,1,0:T(8,128)} %copy-done.10) | copy-start | bytes 3145732

commit v3 on v2

--- a/solution.py
+++ b/solution.py
@@ -13,7 +13,7 @@
 TAPS = 4
 FRAMES = 16
 N_DISH = 4
-CHUNKS = 4
+CHUNKS = (2, 4, 8, 2)
 
 
 full_turn = 2.0 * math.pi
@@ -60,8 +60,8 @@
         preferred_element_type=jnp.float32,
     )
     real, imag = spectrum[:CHB], spectrum[CHB:]
-    gain_real = gain_ref[0, 0].astype(jnp.float32)
-    gain_imag = gain_ref[0, 1].astype(jnp.float32)
+    gain_real = jnp.concatenate([gain_ref[0, 0].astype(jnp.float32)] * frames, axis=1)
+    gain_imag = jnp.concatenate([gain_ref[0, 1].astype(jnp.float32)] * frames, axis=1)
     out_ref[0, 0] = (real * gain_real - imag * gain_imag).astype(jnp.bfloat16)
     out_ref[0, 1] = (real * gain_imag + imag * gain_real).astype(jnp.bfloat16)
 
@@ -174,7 +174,6 @@
     grid_len = grid_rows.shape[1]
     total_dishes = grid_len * dish_count
 
-    step = FRAMES // CHUNKS
     window = jnp.repeat(filter_window().reshape(TAPS, CHA, CHB), 2, axis=1)
     first_index = jnp.arange(CHA, dtype=jnp.int32)
     second_index = jnp.arange(CHB, dtype=jnp.int32)
@@ -197,7 +196,7 @@
         chosen,
         preferred_element_type=jnp.float32,
     ).reshape(dish_rows, 2, CHB, CHA)
-    gains = jnp.tile(gains.astype(jnp.bfloat16), (1, 1, 1, step))
+    gains = gains.astype(jnp.bfloat16)
 
     positions = jnp.arange(grid_len, dtype=jnp.int32)
     tables = jax.vmap(
@@ -213,19 +212,27 @@
     volts = voltages[:, 0].reshape(dish_rows, 2, spans * CHA, CHB)
     volts = jnp.transpose(volts, (0, 2, 1, 3)).reshape(dish_rows, spans, 2 * CHA, CHB)
     total = None
-    for chunk in range(CHUNKS):
+    arrived = None
+    start = 0
+    for step in CHUNKS:
         spectra = channelize(
-            chunk * step, step, volts, window, first_table, turn, second_table, gains
-        )
+            start, step, volts, window, first_table, turn, second_table, gains
+        )
+        start += step
         spectra = spectra.reshape(dish_rows, 2, devices, parts, step * CHA)
         sent = jnp.transpose(spectra, (2, 1, 3, 0, 4))
-        sent, first_table = lax.optimization_barrier((sent, first_table))
+        if arrived is None:
+            sent, first_table = lax.optimization_barrier((sent, first_table))
+        else:
+            sent, first_table, arrived = lax.optimization_barrier((sent, first_table, arrived))
+            power = beam_power(arrived, tables, twist)
+            total = power if total is None else total + power
         gathered = lax.all_to_all(sent, ("freq", "dish"), split_axis=0, concat_axis=0, tiled=True)
-        gathered = gathered.reshape(block_count, dish_count, 2, parts, dish_rows, step * CHA)
-        power = beam_power(gathered, tables, twist)
-        total = power if total is None else total + power
+        arrived = gathered.reshape(block_count, dish_count, 2, parts, dish_rows, step * CHA)
+    total = total + beam_power(arrived, tables, twist)
+    total = total.astype(jnp.bfloat16)
     out = lax.all_to_all(total, "dish", split_axis=0, concat_axis=0, tiled=True)
-    return out.reshape(block_width, grid_len)
+    return out.reshape(block_width, grid_len).astype(jnp.float32)
 
 
 def solution(mesh):

time: 506 us -> 462 us (0.913)
  local copies, waits for them, and re-layouts: 107 us -> 70.1 us
  starting transfers between devices: 30.3 us -> 19.9 us
  blocking collectives: 16.9 us -> 11.2 us
    unnamed x28 -> x19, local copies, waits for them, and re-layouts: 19.6 us -> 7.26 us
    reshape x8 -> x6, local copies, waits for them, and re-layouts: 62.5 us -> 51.4 us  [body(): spectra = spectra.reshape(dish_rows, 2, devices, parts, step * CHA)]
    another operation x2 -> x0, local copies, waits for them, and re-layouts: 10.7 us -> none  [body(): gains = jnp.tile(gains.astype(jnp.bfloat16), (1, 1, 1, step))]
    all_to_all x4, starting transfers between devices: 30.3 us -> 19.9 us  [body(): lax.all_to_all(sent, ('freq', 'dish'), split_axis=0, concat_axis=0, tiled...]
    all_to_all x1, blocking collectives: 16.9 us -> 11.2 us  [body(): out = lax.all_to_all(total, 'dish', split_axis=0, concat_axis=0, tiled=True)]
    all_to_all x4, waiting for transfers between devices: 205 us -> 210 us  [body(): lax.all_to_all(sent, ('freq', 'dish'), split_axis=0, concat_axis=0, tiled...]
  transfers between devices with their start and end apart: 4 -> 4, of which waited for: 4 -> 4; matrix products, arithmetic and copies ran while one was open for 13% -> 14% of each run, Pallas kernels for 18% -> 21%
where the time goes in v3:
time: 462 us; the launch traced here: 454 us
  waiting for transfers between devices  210 us (45%)
  Pallas kernels  124 us (27%)
  local copies, waits for them, and re-layouts  70.1 us (15%)
  starting transfers between devices  19.9 us (4%)
  other arithmetic  15 us (3%)
  blocking collectives  11.2 us (2%)
    all_to_all x4, waiting for transfers between devices, body(): lax.all_to_all(sent, ('freq', 'dish'), split_axis=0, concat_axis=0, tiled...  210 us
    pallas_call x4, Pallas kernels, channelize(): pl.pallas_call(lambda *refs: channel_kernel(start, frames, *refs), grid=(...  100 us
    reshape x6, local copies, waits for them, and re-layouts, body(): spectra = spectra.reshape(dish_rows, 2, devices, parts, step * CHA)  51.4 us
    pallas_call x4, Pallas kernels, beam_power(): pl.pallas_call(lambda *refs: beam_kernel(1.0 / (N_DISH * FRAMES), *refs),...  24.2 us
    all_to_all x4, starting transfers between devices, body(): lax.all_to_all(sent, ('freq', 'dish'), split_axis=0, concat_axis=0, tiled...  19.9 us
    all_to_all x1, blocking collectives, body(): out = lax.all_to_all(total, 'dish', split_axis=0, concat_axis=0, tiled=True)  11.2 us
  transfers between devices with their start and end apart: 4, of which 4 were waited for; matrix products, arithmetic and copies ran while one was open for 14% of the time, Pallas kernels for 21%

profile of v3, /device:TPU:0, one launch (start us, length us, event | category | flops | bytes accessed | tf_op | source)
XLA Modules:
  0.0 453.5 jit_solution(3159007554825626256)
XLA Ops:
  0.0 0.7 broadcast_multiply_fusion
  0.9 0.3 multiply_convert_fusion.2
  1.2 0.3 fusion.57
  1.5 0.2 multiply_convert_fusion.4
  1.6 0.1 fusion.58
  1.8 0.1 fusion.55
  1.9 1.3 fusion.30
  3.2 0.1 copy.27
  3.8 0.8 reshape_squeeze.7
  4.6 1.5 fusion
  6.1 2.9 convert_element_type.199.refs_5_
  9.7 0.6 fusion.36
  10.4 24.2 %shard_map.46 = bf16[32,2,128,128]{3,2,1,0:T(8,128)(2,1)S(1)} custom-call(bf16[32,19,128,128]{3,2,1,0:T(8,128)(2,1)} %bitcast.76, f32[4,128,128]{2,1,0:T(8,128)S(1)} %bitcast.68, bf16[128,128]{1,0:T(8,128)(2,1)S(1)} %copy.28.refs_2_, f32[2,64,128]{2,1,0:T(8,128)S(1)} %pad_maximum_fusion.refs_3_, bf16[256,256]{1,0:T(8,128)(2,1)S(1)} %bitcast.72, ...), custom_call_target="tpu_custom_call" | custom-call | flops 805306368 | bytes 23068672 | tf_op jit(solution)/shard_map/pallas_call | solution.py:80
  34.7 3.8 copy.53
  38.5 7.6 %all-to-all-start = ((bf16[32,2,4,32,128]{4,3,2,1,0:T(8,128)(2,1)}), bf16[32,2,4,32,128]{4,3,2,1,0:T(8,128)(2,1)}, u32[]{:S(2)}, u32[]{:S(2)}) async-start(bf16[32,2,4,32,128]{4,3,2,1,0:T(8,128)(2,1)} %bitcast.82), calls=%async_computation | async-start | bytes 4194304 | tf_op jit(solution)/shard_map/all_to_all | solution.py:230
  46.2 25.0 %shard_map.47 = bf16[32,2,128,256]{3,2,1,0:T(8,128)(2,1)S(1)} custom-call(bf16[32,19,128,128]{3,2,1,0:T(8,128)(2,1)} %bitcast.77, f32[4,128,128]{2,1,0:T(8,128)S(1)} %bitcast.69, bf16[128,128]{1,0:T(8,128)(2,1)S(1)} %copy.30.refs_2_, f32[2,64,128]{2,1,0:T(8,128)S(1)} %pad_maximum_fusion.refs_3_, bf16[256,256]{1,0:T(8,128)(2,1)S(1)} %bitcast.73, ...), custom_call_target="tpu_custom_call" | custom-call | flops 1610612736 | bytes 25165824 | tf_op jit(solution)/shard_map/pallas_call | solution.py:80
  71.2 2.0 copy-done.1
  73.2 6.9 %reshape.489 = bf16[32,2,32,4,256]{4,3,2,1,0:T(4,128)(2,1)} reshape(bf16[32,2,128,256]{3,2,1,0:T(8,128)(2,1)} %copy-done.1) | data formatting | bytes 8388608 | tf_op jit(solution)/shard_map/reshape | solution.py:222
  80.1 8.7 %copy.51 = bf16[32,2,32,4,256]{4,0,3,1,2:T(8,128)(2,1)} copy(bf16[32,2,32,4,256]{4,3,2,1,0:T(4,128)(2,1)} %reshape.489) | data formatting | bytes 8388608 | tf_op jit(solution)/shard_map/reshape | solution.py:222
  88.8 6.2 %all-to-all-done = bf16[32,2,4,32,128]{4,3,2,1,0:T(8,128)(2,1)} async-done(((bf16[32,2,4,32,128]{4,3,2,1,0:T(8,128)(2,1)}), bf16[32,2,4,32,128]{4,3,2,1,0:T(8,128)(2,1)}, u32[]{:S(2)}, u32[]{:S(2)}) %all-to-all-start) | async-done | bytes 2097184 | tf_op jit(solution)/shard_map/all_to_all | solution.py:230
  95.0 4.4 all-to-all-start.1
  99.4 26.6 %shard_map.49 = bf16[32,2,128,512]{3,2,1,0:T(8,128)(2,1)S(1)} custom-call(bf16[32,19,128,128]{3,2,1,0:T(8,128)(2,1)} %bitcast.78, f32[4,128,128]{2,1,0:T(8,128)S(1)} %bitcast.70, bf16[128,128]{1,0:T(8,128)(2,1)S(1)} %copy.34.refs_2_, f32[2,64,128]{2,1,0:T(8,128)S(1)} %pad_maximum_fusion.refs_3_, bf16[256,256]{1,0:T(8,128)(2,1)S(1)} %bitcast.74, ...), custom_call_target="tpu_custom_call" | custom-call | flops 3221225472 | bytes 29360128 | tf_op jit(solution)/shard_map/pallas_call | solution.py:80
  126.1 3.2 copy-done
  129.3 12.6 %reshape.492 = bf16[32,2,32,4,512]{4,3,2,1,0:T(4,128)(2,1)} reshape(bf16[32,2,128,512]{3,2,1,0:T(8,128)(2,1)} %copy-done) | data formatting | bytes 16777216 | tf_op jit(solution)/shard_map/reshape | solution.py:222
  141.9 15.7 %copy.50 = bf16[32,2,32,4,512]{4,0,3,1,2:T(8,128)(2,1)} copy(bf16[32,2,32,4,512]{4,3,2,1,0:T(4,128)(2,1)} %reshape.492) | data formatting | bytes 16777216 | tf_op jit(solution)/shard_map/reshape | solution.py:222
  157.5 35.7 %all-to-all-done.1 = bf16[32,2,4,32,256]{4,3,2,1,0:T(8,128)(2,1)} async-done(((bf16[32,2,4,32,256]{4,3,2,1,0:T(8,128)(2,1)}), bf16[32,2,4,32,256]{4,3,2,1,0:T(8,128)(2,1)}, u32[]{:S(2)}, u32[]{:S(2)}) %all-to-all-start.1) | async-done | bytes 4194336 | tf_op jit(solution)/shard_map/all_to_all | solution.py:230
  193.2 4.3 all-to-all-start.2
  197.7 24.3 %shard_map.51 = bf16[32,2,128,128]{3,2,1,0:T(8,128)(2,1)S(1)} custom-call(bf16[32,19,128,128]{3,2,1,0:T(8,128)(2,1)} %bitcast.79, f32[4,128,128]{2,1,0:T(8,128)S(1)} %bitcast.71, bf16[128,128]{1,0:T(8,128)(2,1)S(1)} %copy.36.refs_2_, f32[2,64,128]{2,1,0:T(8,128)S(1)} %pad_maximum_fusion.refs_3_, bf16[256,256]{1,0:T(8,128)(2,1)S(1)} %bitcast.75, ...), custom_call_target="tpu_custom_call" | custom-call | flops 805306368 | bytes 23068672 | tf_op jit(solution)/shard_map/pallas_call | solution.py:80
  221.9 3.8 copy.52
  225.7 157.9 %all-to-all-done.2 = bf16[32,2,4,32,512]{4,3,2,1,0:T(8,128)(2,1)} async-done(((bf16[32,2,4,32,512]{4,3,2,1,0:T(8,128)(2,1)}), bf16[32,2,4,32,512]{4,3,2,1,0:T(8,128)(2,1)}, u32[]{:S(2)}, u32[]{:S(2)}) %all-to-all-start.2) | async-done | bytes 8388640 | tf_op jit(solution)/shard_map/all_to_all | solution.py:230
  383.6 3.6 all-to-all-start.3
  387.2 4.3 fusion.7
  391.6 5.0 %multiply_convert_fusion = (bf16[4,256,1,256]{3,1,2,0:T(8,128)(2,1)S(1)}, bf16[4,256,1,256]{3,1,2,0:T(8,128)(2,1)S(1)}) fusion(s32[4,256]{1,0:T(4,128)S(1)} %copy-done.7), kind=kLoop, calls=%fused_computation.16 | loop fusion | flops 4718592 | bytes 1052672 | tf_op jit(solution)/shard_map/vmap()/convert_element_type | solution.py:26
  396.6 0.1 maximum_bitcast_fusion.1
  396.8 0.2 maximum_bitcast_fusion
  397.0 3.6 copy.32
  400.5 3.2 reshape.491.refs_1_
  403.7 0.1 fusion.65
  403.9 4.1 shard_map.48
  408.0 5.8 %shard_map.50 = f32[4,256,256]{2,1,0:T(8,128)S(1)} custom-call(bf16[8,4,2,4,32,256]{5,4,3,2,1,0:T(8,128)(2,1)} %bitcast.23.refs_0_, bf16[4,2,256,512]{3,2,1,0:T(8,128)(2,1)S(1)} %reshape.491.refs_1_, f32[4,2,256]{2,1,0:T(2,128)S(1)} %pad_maximum_fusion.1.refs_2_), custom_call_target="tpu_custom_call" | custom-call | flops 2147483648 | bytes 6291456 | tf_op jit(solution)/shard_map/pallas_call | solution.py:148
  413.9 1.0 copy-done.2
  414.9 9.9 %shard_map.52 = f32[4,256,256]{2,1,0:T(8,128)S(1)} custom-call(bf16[8,4,2,4,32,512]{5,4,3,2,1,0:T(8,128)(2,1)} %bitcast.26.refs_0_, bf16[4,2,256,512]{3,2,1,0:T(8,128)(2,1)S(1)} %reshape.491.refs_1_, f32[4,2,256]{2,1,0:T(2,128)S(1)} %pad_maximum_fusion.1.refs_2_), custom_call_target="tpu_custom_call" | custom-call | flops 4294967296 | bytes 10485760 | tf_op jit(solution)/shard_map/pallas_call | solution.py:148
  424.9 1.0 copy-done.4
  425.8 10.3 %all-to-all-done.3 = bf16[32,2,4,32,128]{4,3,2,1,0:T(8,128)(2,1)} async-done(((bf16[32,2,4,32,128]{4,3,2,1,0:T(8,128)(2,1)}), bf16[32,2,4,32,128]{4,3,2,1,0:T(8,128)(2,1)}, u32[]{:S(2)}, u32[]{:S(2)}) %all-to-all-start.3) | async-done | bytes 2097184 | tf_op jit(solution)/shard_map/all_to_all | solution.py:230
  436.1 4.3 shard_map.53
  440.4 0.3 add_convert_fusion
  440.8 11.2 %all_to_all.25 = bf16[4,256,256]{2,1,0:T(8,128)(2,1)S(1)} all-to-all(bf16[4,256,256]{2,1,0:T(8,128)(2,1)S(1)} %add_convert_fusion), channel_id=1, replica_groups=mesh['freq'=8,'dish'=4] {'dish'}, dimensions={0} | all-to-all | bytes 1048576 | tf_op jit(solution)/shard_map/all_to_all | solution.py:234
  452.0 1.1 bitcast_convert_fusion
  (31 shorter events, 1.0 us)
Async XLA Ops:
  0.0 4.6 %copy-start.8 = (s32[8]{0:T(128)S(1)}, s32[8]{0:T(128)}, u32[]{:S(2)}) copy-start(s32[8]{0:T(128)} %param.6) | copy-start | bytes 100
  0.0 3.7 copy-start.6
  38.5 56.5 %all-to-all-start = ((bf16[32,2,4,32,128]{4,3,2,1,0:T(8,128)(2,1)}), bf16[32,2,4,32,128]{4,3,2,1,0:T(8,128)(2,1)}, u32[]{:S(2)}, u32[]{:S(2)}) async-start(bf16[32,2,4,32,128]{4,3,2,1,0:T(8,128)(2,1)} %bitcast.82), calls=%async_computation | async-start | bytes 4194304 | tf_op jit(solution)/shard_map/all_to_all | solution.py:230
  71.2 2.0 copy-start.1
  95.0 98.3 %all-to-all-start.1 = ((bf16[32,2,4,32,256]{4,3,2,1,0:T(8,128)(2,1)}), bf16[32,2,4,32,256]{4,3,2,1,0:T(8,128)(2,1)}, u32[]{:S(2)}, u32[]{:S(2)}) async-start(bf16[32,2,4,32,256]{4,3,2,1,0:T(8,128)(2,1)} %bitcast.81), calls=%async_computation.1 | async-start | bytes 8388608 | tf_op jit(solution)/shard_map/all_to_all | solution.py:230
  126.1 3.2 copy-start
  193.2 190.3 %all-to-all-start.2 = ((bf16[32,2,4,32,512]{4,3,2,1,0:T(8,128)(2,1)}), bf16[32,2,4,32,512]{4,3,2,1,0:T(8,128)(2,1)}, u32[]{:S(2)}, u32[]{:S(2)}) async-start(bf16[32,2,4,32,512]{4,3,2,1,0:T(8,128)(2,1)} %bitcast.80), calls=%async_computation.2 | async-start | bytes 16777216 | tf_op jit(solution)/shard_map/all_to_all | solution.py:230
  383.6 3.6 copy-start.7
  383.6 52.5 %all-to-all-start.3 = ((bf16[32,2,4,32,128]{4,3,2,1,0:T(8,128)(2,1)}), bf16[32,2,4,32,128]{4,3,2,1,0:T(8,128)(2,1)}, u32[]{:S(2)}, u32[]{:S(2)}) async-start(bf16[32,2,4,32,128]{4,3,2,1,0:T(8,128)(2,1)} %bitcast.63), calls=%async_computation.3 | async-start | bytes 4194304 | tf_op jit(solution)/shard_map/all_to_all | solution.py:230
  413.8 1.1 copy-start.2
  424.9 1.0 copy-start.4
  436.1 4.3 copy-start.3
  436.1 4.3 copy-start.5

commit v4 on v3

--- a/solution.py
+++ b/solution.py
@@ -81,7 +81,9 @@
         lambda *refs: channel_kernel(start, frames, *refs),
         grid=(feeds,),
         in_specs=[
-            own(volts),
+            pl.BlockSpec(
+                (1, start + frames + TAPS - 1) + volts.shape[2:], lambda r: (r, 0, 0, 0)
+            ),
             whole(window),
             whole(first_table),
             whole(turn),
@@ -93,7 +95,7 @@
         compiler_params=pltpu.CompilerParams(vmem_limit_bytes=32 * 2**20),
         cost_estimate=pl.CostEstimate(
             flops=feeds * frames * (2 * 128**3 + 2 * 64 * 256 * 256),
-            bytes_accessed=volts.size * 2 + gains.size * 2 + feeds * 512 * width,
+            bytes_accessed=feeds * (start + frames + 3) * 2**15 + gains.size * 2 + feeds * 512 * width,
             transcendentals=0,
         ),
     )(volts, window, first_table, turn, second_table, gains)

time: 462 us -> 459 us (level)
  Pallas kernels: 124 us -> 119 us
    pallas_call x4, Pallas kernels: 100 us -> 94.5 us  [channelize(): pl.pallas_call(lambda *refs: channel_kernel(start, frames, *refs), grid=(...]
where the time goes in v4:
time: 459 us; the launch traced here: 451 us
  waiting for transfers between devices  213 us (46%)
  Pallas kernels  119 us (26%)
  local copies, waits for them, and re-layouts  70.1 us (15%)
  starting transfers between devices  19.9 us (4%)
  other arithmetic  15 us (3%)
  blocking collectives  11.2 us (2%)
    all_to_all x4, waiting for transfers between devices, body(): lax.all_to_all(sent, ('freq', 'dish'), split_axis=0, concat_axis=0, tiled...  213 us
    pallas_call x4, Pallas kernels, channelize(): pl.pallas_call(lambda *refs: channel_kernel(start, frames, *refs), grid=(...  94.5 us
    reshape x6, local copies, waits for them, and re-layouts, body(): spectra = spectra.reshape(dish_rows, 2, devices, parts, step * CHA)  51.4 us
    pallas_call x4, Pallas kernels, beam_power(): pl.pallas_call(lambda *refs: beam_kernel(1.0 / (N_DISH * FRAMES), *refs),...  24.2 us
    all_to_all x4, starting transfers between devices, body(): lax.all_to_all(sent, ('freq', 'dish'), split_axis=0, concat_axis=0, tiled...  19.9 us
    all_to_all x1, blocking collectives, body(): out = lax.all_to_all(total, 'dish', split_axis=0, concat_axis=0, tiled=True)  11.2 us
  transfers between devices with their start and end apart: 4, of which 4 were waited for; matrix products, arithmetic and copies ran while one was open for 14% of the time, Pallas kernels for 21%

profile of v4, /device:TPU:0, one launch (start us, length us, event | category | flops | bytes accessed | tf_op | source)
XLA Modules:
  0.0 450.5 jit_solution(11194829754036263628)
XLA Ops:
  0.0 0.7 broadcast_multiply_fusion
  0.9 0.3 multiply_convert_fusion.2
  1.2 0.3 fusion.57
  1.5 0.2 multiply_convert_fusion.4
  1.6 0.1 fusion.58
  1.8 0.1 fusion.55
  1.9 1.3 fusion.30
  3.2 0.1 copy.27
  3.8 0.8 reshape_squeeze.7
  4.6 1.5 fusion
  6.1 2.9 convert_element_type.199.refs_5_
  9.7 0.6 fusion.36
  10.4 21.3 %shard_map.46 = bf16[32,2,128,128]{3,2,1,0:T(8,128)(2,1)S(1)} custom-call(bf16[32,19,128,128]{3,2,1,0:T(8,128)(2,1)} %bitcast.76, f32[4,128,128]{2,1,0:T(8,128)S(1)} %bitcast.68, bf16[128,128]{1,0:T(8,128)(2,1)S(1)} %copy.28.refs_2_, f32[2,64,128]{2,1,0:T(8,128)S(1)} %pad_maximum_fusion.refs_3_, bf16[256,256]{1,0:T(8,128)(2,1)S(1)} %bitcast.72, ...), custom_call_target="tpu_custom_call" | custom-call | flops 805306368 | bytes 8388608 | tf_op jit(solution)/shard_map/pallas_call | solution.py:80
  31.7 3.8 copy.53
  35.5 7.6 %all-to-all-start = ((bf16[32,2,4,32,128]{4,3,2,1,0:T(8,128)(2,1)}), bf16[32,2,4,32,128]{4,3,2,1,0:T(8,128)(2,1)}, u32[]{:S(2)}, u32[]{:S(2)}) async-start(bf16[32,2,4,32,128]{4,3,2,1,0:T(8,128)(2,1)} %bitcast.82), calls=%async_computation | async-start | bytes 4194304 | tf_op jit(solution)/shard_map/all_to_all | solution.py:232
  43.2 22.8 %shard_map.47 = bf16[32,2,128,256]{3,2,1,0:T(8,128)(2,1)S(1)} custom-call(bf16[32,19,128,128]{3,2,1,0:T(8,128)(2,1)} %bitcast.77, f32[4,128,128]{2,1,0:T(8,128)S(1)} %bitcast.69, bf16[128,128]{1,0:T(8,128)(2,1)S(1)} %copy.30.refs_2_, f32[2,64,128]{2,1,0:T(8,128)S(1)} %pad_maximum_fusion.refs_3_, bf16[256,256]{1,0:T(8,128)(2,1)S(1)} %bitcast.73, ...), custom_call_target="tpu_custom_call" | custom-call | flops 1610612736 | bytes 14680064 | tf_op jit(solution)/shard_map/pallas_call | solution.py:80
  66.0 2.0 copy-done.1
  68.0 6.9 %reshape.489 = bf16[32,2,32,4,256]{4,3,2,1,0:T(4,128)(2,1)} reshape(bf16[32,2,128,256]{3,2,1,0:T(8,128)(2,1)} %copy-done.1) | data formatting | bytes 8388608 | tf_op jit(solution)/shard_map/reshape | solution.py:224
  74.9 8.7 %copy.51 = bf16[32,2,32,4,256]{4,0,3,1,2:T(8,128)(2,1)} copy(bf16[32,2,32,4,256]{4,3,2,1,0:T(4,128)(2,1)} %reshape.489) | data formatting | bytes 8388608 | tf_op jit(solution)/shard_map/reshape | solution.py:224
  83.7 8.3 %all-to-all-done = bf16[32,2,4,32,128]{4,3,2,1,0:T(8,128)(2,1)} async-done(((bf16[32,2,4,32,128]{4,3,2,1,0:T(8,128)(2,1)}), bf16[32,2,4,32,128]{4,3,2,1,0:T(8,128)(2,1)}, u32[]{:S(2)}, u32[]{:S(2)}) %all-to-all-start) | async-done | bytes 2097184 | tf_op jit(solution)/shard_map/all_to_all | solution.py:232
  92.0 4.4 all-to-all-start.1
  96.5 26.2 %shard_map.49 = bf16[32,2,128,512]{3,2,1,0:T(8,128)(2,1)S(1)} custom-call(bf16[32,19,128,128]{3,2,1,0:T(8,128)(2,1)} %bitcast.78, f32[4,128,128]{2,1,0:T(8,128)S(1)} %bitcast.70, bf16[128,128]{1,0:T(8,128)(2,1)S(1)} %copy.34.refs_2_, f32[2,64,128]{2,1,0:T(8,128)S(1)} %pad_maximum_fusion.refs_3_, bf16[256,256]{1,0:T(8,128)(2,1)S(1)} %bitcast.74, ...), custom_call_target="tpu_custom_call" | custom-call | flops 3221225472 | bytes 27262976 | tf_op jit(solution)/shard_map/pallas_call | solution.py:80
  122.7 3.2 copy-done
  125.9 12.6 %reshape.492 = bf16[32,2,32,4,512]{4,3,2,1,0:T(4,128)(2,1)} reshape(bf16[32,2,128,512]{3,2,1,0:T(8,128)(2,1)} %copy-done) | data formatting | bytes 16777216 | tf_op jit(solution)/shard_map/reshape | solution.py:224
  138.4 15.7 %copy.50 = bf16[32,2,32,4,512]{4,0,3,1,2:T(8,128)(2,1)} copy(bf16[32,2,32,4,512]{4,3,2,1,0:T(4,128)(2,1)} %reshape.492) | data formatting | bytes 16777216 | tf_op jit(solution)/shard_map/reshape | solution.py:224
  154.1 36.2 %all-to-all-done.1 = bf16[32,2,4,32,256]{4,3,2,1,0:T(8,128)(2,1)} async-done(((bf16[32,2,4,32,256]{4,3,2,1,0:T(8,128)(2,1)}), bf16[32,2,4,32,256]{4,3,2,1,0:T(8,128)(2,1)}, u32[]{:S(2)}, u32[]{:S(2)}) %all-to-all-start.1) | async-done | bytes 4194336 | tf_op jit(solution)/shard_map/all_to_all | solution.py:232
  190.3 4.3 all-to-all-start.2
  194.7 24.3 %shard_map.51 = bf16[32,2,128,128]{3,2,1,0:T(8,128)(2,1)S(1)} custom-call(bf16[32,19,128,128]{3,2,1,0:T(8,128)(2,1)} %bitcast.79, f32[4,128,128]{2,1,0:T(8,128)S(1)} %bitcast.71, bf16[128,128]{1,0:T(8,128)(2,1)S(1)} %copy.36.refs_2_, f32[2,64,128]{2,1,0:T(8,128)S(1)} %pad_maximum_fusion.refs_3_, bf16[256,256]{1,0:T(8,128)(2,1)S(1)} %bitcast.75, ...), custom_call_target="tpu_custom_call" | custom-call | flops 805306368 | bytes 23068672 | tf_op jit(solution)/shard_map/pallas_call | solution.py:80
  218.9 3.8 copy.52
  222.7 157.9 %all-to-all-done.2 = bf16[32,2,4,32,512]{4,3,2,1,0:T(8,128)(2,1)} async-done(((bf16[32,2,4,32,512]{4,3,2,1,0:T(8,128)(2,1)}), bf16[32,2,4,32,512]{4,3,2,1,0:T(8,128)(2,1)}, u32[]{:S(2)}, u32[]{:S(2)}) %all-to-all-start.2) | async-done | bytes 8388640 | tf_op jit(solution)/shard_map/all_to_all | solution.py:232
  380.6 3.6 all-to-all-start.3
  384.2 4.3 fusion.7
  388.6 5.0 %multiply_convert_fusion = (bf16[4,256,1,256]{3,1,2,0:T(8,128)(2,1)S(1)}, bf16[4,256,1,256]{3,1,2,0:T(8,128)(2,1)S(1)}) fusion(s32[4,256]{1,0:T(4,128)S(1)} %copy-done.7), kind=kLoop, calls=%fused_computation.16 | loop fusion | flops 4718592 | bytes 1052672 | tf_op jit(solution)/shard_map/vmap()/convert_element_type | solution.py:26
  393.6 0.1 maximum_bitcast_fusion.1
  393.8 0.2 maximum_bitcast_fusion
  394.0 3.6 copy.32
  397.5 3.2 reshape.491.refs_1_
  400.7 0.1 fusion.65
  400.9 4.1 shard_map.48
  405.0 5.8 %shard_map.50 = f32[4,256,256]{2,1,0:T(8,128)S(1)} custom-call(bf16[8,4,2,4,32,256]{5,4,3,2,1,0:T(8,128)(2,1)} %bitcast.23.refs_0_, bf16[4,2,256,512]{3,2,1,0:T(8,128)(2,1)S(1)} %reshape.491.refs_1_, f32[4,2,256]{2,1,0:T(2,128)S(1)} %pad_maximum_fusion.1.refs_2_), custom_call_target="tpu_custom_call" | custom-call | flops 2147483648 | bytes 6291456 | tf_op jit(solution)/shard_map/pallas_call | solution.py:150
  410.9 1.0 copy-done.2
  411.9 9.9 %shard_map.52 = f32[4,256,256]{2,1,0:T(8,128)S(1)} custom-call(bf16[8,4,2,4,32,512]{5,4,3,2,1,0:T(8,128)(2,1)} %bitcast.26.refs_0_, bf16[4,2,256,512]{3,2,1,0:T(8,128)(2,1)S(1)} %reshape.491.refs_1_, f32[4,2,256]{2,1,0:T(2,128)S(1)} %pad_maximum_fusion.1.refs_2_), custom_call_target="tpu_custom_call" | custom-call | flops 4294967296 | bytes 10485760 | tf_op jit(solution)/shard_map/pallas_call | solution.py:150
  421.9 1.0 copy-done.4
  422.9 10.3 %all-to-all-done.3 = bf16[32,2,4,32,128]{4,3,2,1,0:T(8,128)(2,1)} async-done(((bf16[32,2,4,32,128]{4,3,2,1,0:T(8,128)(2,1)}), bf16[32,2,4,32,128]{4,3,2,1,0:T(8,128)(2,1)}, u32[]{:S(2)}, u32[]{:S(2)}) %all-to-all-start.3) | async-done | bytes 2097184 | tf_op jit(solution)/shard_map/all_to_all | solution.py:232
  433.2 4.3 shard_map.53
  437.5 0.3 add_convert_fusion
  437.8 11.2 %all_to_all.25 = bf16[4,256,256]{2,1,0:T(8,128)(2,1)S(1)} all-to-all(bf16[4,256,256]{2,1,0:T(8,128)(2,1)S(1)} %add_convert_fusion), channel_id=1, replica_groups=mesh['freq'=8,'dish'=4] {'dish'}, dimensions={0} | all-to-all | bytes 1048576 | tf_op jit(solution)/shard_map/all_to_all | solution.py:236
  449.0 1.1 bitcast_convert_fusion
  (31 shorter events, 1.0 us)
Async XLA Ops:
  0.0 4.6 %copy-start.8 = (s32[8]{0:T(128)S(1)}, s32[8]{0:T(128)}, u32[]{:S(2)}) copy-start(s32[8]{0:T(128)} %param.6) | copy-start | bytes 100
  0.0 3.7 copy-start.6
  35.5 56.5 %all-to-all-start = ((bf16[32,2,4,32,128]{4,3,2,1,0:T(8,128)(2,1)}), bf16[32,2,4,32,128]{4,3,2,1,0:T(8,128)(2,1)}, u32[]{:S(2)}, u32[]{:S(2)}) async-start(bf16[32,2,4,32,128]{4,3,2,1,0:T(8,128)(2,1)} %bitcast.82), calls=%async_computation | async-start | bytes 4194304 | tf_op jit(solution)/shard_map/all_to_all | solution.py:232
  66.0 2.0 copy-start.1
  92.0 98.3 %all-to-all-start.1 = ((bf16[32,2,4,32,256]{4,3,2,1,0:T(8,128)(2,1)}), bf16[32,2,4,32,256]{4,3,2,1,0:T(8,128)(2,1)}, u32[]{:S(2)}, u32[]{:S(2)}) async-start(bf16[32,2,4,32,256]{4,3,2,1,0:T(8,128)(2,1)} %bitcast.81), calls=%async_computation.1 | async-start | bytes 8388608 | tf_op jit(solution)/shard_map/all_to_all | solution.py:232
  122.7 3.2 copy-start
  190.3 190.3 %all-to-all-start.2 = ((bf16[32,2,4,32,512]{4,3,2,1,0:T(8,128)(2,1)}), bf16[32,2,4,32,512]{4,3,2,1,0:T(8,128)(2,1)}, u32[]{:S(2)}, u32[]{:S(2)}) async-start(bf16[32,2,4,32,512]{4,3,2,1,0:T(8,128)(2,1)} %bitcast.80), calls=%async_computation.2 | async-start | bytes 16777216 | tf_op jit(solution)/shard_map/all_to_all | solution.py:232
  380.6 3.6 copy-start.7
  380.6 52.5 %all-to-all-start.3 = ((bf16[32,2,4,32,128]{4,3,2,1,0:T(8,128)(2,1)}), bf16[32,2,4,32,128]{4,3,2,1,0:T(8,128)(2,1)}, u32[]{:S(2)}, u32[]{:S(2)}) async-start(bf16[32,2,4,32,128]{4,3,2,1,0:T(8,128)(2,1)} %bitcast.63), calls=%async_computation.3 | async-start | bytes 4194304 | tf_op jit(solution)/shard_map/all_to_all | solution.py:232
  410.9 1.1 copy-start.2
  421.9 1.0 copy-start.4
  433.1 4.3 copy-start.3
  433.2 4.3 copy-start.5
